TPU v7x, 32 devices: a whole 2x2x4 slice. The times are simulated.
32 devices in a mesh: groups: 2 (over x), fsdp: 4 (over y, core), tensor: 4 (over z).
Axes of the slice: x: 2, y: 2, z: 4, core: 2. Of those that a mesh axis runs over, the one named last changes fastest.
Arguments:
- tokens: bfloat16 [8192, 5120], P(('groups', 'fsdp', 'tensor')), parts along dimension 0, may hold values from -6 to 6
- w_qkv: bfloat16 [10240, 6144], P(('groups', 'fsdp', 'tensor')), parts along dimension 0, may hold values from -0.078125 to 0.078125
- norm_gain: float32 [5120], replicated, may hold values from 0.1 to 1.9
- q_gain: float32 [128], replicated, may hold values from 0.5 to 3
- k_gain: float32 [128], replicated, may hold values from 0.5 to 3
- lengths: int32 [8], P(('groups', 'fsdp')), parts along dimension 0, may hold values from 256 to 1024, as said below
Outputs:
- attended: bfloat16 [8192, 4096], P(('groups', 'fsdp'), 'tensor'), parts along dimension 0
There are 2 independent parts, one for each index of `groups`. A program takes and returns all parts, laid end to end along the dimension named above; an argument that names none is the same for every part. Nothing has to cross between parts.
Inputs may be any that keep to these rules, and one draw needn't show every extreme that they name: `lengths`: one prompt has the full length 1024.
All inputs are finite; a program needn't handle non-finite values.
Results may differ from a plain program's by a relative error of at most 0.012.
The roundings to bfloat16 on the way count: a program that leaves them out, or rounds other values in their place, can miss the bound.
Values may be sent and summed in bfloat16 or wider, within the bound.
No kernel may reach another device: no remote copies, remote signals or barrier semaphores. Data moves between devices by JAX's collectives and lax.ppermute only.
A program may use at most 192 MiB of HBM per device.

v0:
```python
import functools
import jax
import jax.numpy as jnp
from jax import lax
from jax.experimental import pallas as pl
from jax.experimental.pallas import tpu as pltpu
from jax.sharding import PartitionSpec as P

KV = 8
HD = 128
GQ = 4
LOG2E = 1.4426950408889634
VMEM_BYTES = 48 * 1024 * 1024


def head_norm(vec, gain):
    scale = lax.rsqrt(jnp.mean(vec * vec, axis=-1, keepdims=True) + 1e-06)
    return vec * scale * gain


def angles(positions):
    half = HD // 2
    freqs = 1000000.0 ** (-2.0 * jnp.arange(half, dtype=jnp.float32) / HD)
    return positions.astype(jnp.float32)[:, None] * freqs[None, :]


def rotate(vec, positions):
    half = vec.shape[-1] // 2
    angle = angles(positions)
    cosine = jnp.cos(angle)[:, None, None, :]
    sine = jnp.sin(angle)[:, None, None, :]
    first = vec[..., :half]
    second = vec[..., half:]
    return jnp.concatenate(
        [first * cosine - second * sine, second * cosine + first * sine], axis=-1
    )


def attend(qkv, q_gain, k_gain, length):
    rows = qkv.shape[0]
    group = qkv.shape[2] - 2
    positions = jnp.arange(rows, dtype=jnp.int32)
    query = rotate(head_norm(qkv[:, :, :group], q_gain), positions).astype(jnp.bfloat16)
    keyed = rotate(head_norm(qkv[:, :, group : group + 1], k_gain), positions)[:, :, 0].astype(
        jnp.bfloat16
    )
    value = qkv[:, :, group + 1].astype(jnp.bfloat16)
    scores = jnp.einsum(
        "ikgd,jkd->kgij", query, keyed, preferred_element_type=jnp.float32
    ) / jnp.sqrt(jnp.float32(qkv.shape[3]))
    allowed = (positions[None, :] <= positions[:, None]) & (positions[None, :] < length)
    scores = jnp.where(allowed[None, None], scores, jnp.float32(-1e30))
    top = jnp.max(scores, axis=-1, keepdims=True)
    weights = jnp.exp(scores - top)
    probs = (weights / jnp.sum(weights, axis=-1, keepdims=True)).astype(jnp.bfloat16)
    out = jnp.einsum("kgij,jkd->ikgd", probs, value, preferred_element_type=jnp.float32)
    return out.reshape(rows, -1).astype(jnp.bfloat16)


def any_mesh(tokens, w_qkv, norm_gain, q_gain, k_gain, lengths):
    tensor_count = lax.axis_size("tensor")
    moved = lax.all_to_all(w_qkv, "tensor", split_axis=1, concat_axis=0, tiled=True)
    weight_cols = lax.all_gather(moved, "fsdp", axis=0, tiled=True)
    normed = head_norm(tokens.astype(jnp.float32), norm_gain).astype(jnp.bfloat16)
    qkv = jnp.dot(
        lax.all_gather(normed, "tensor", axis=0, tiled=True),
        weight_cols,
        preferred_element_type=jnp.float32,
    )
    qkv = qkv.reshape(qkv.shape[0], KV // tensor_count, GQ + 2, HD)
    return attend(qkv, q_gain, k_gain, lengths[0])


def project_kernel(counts, sources, tile, scal, *refs):
    blocks = len(counts)
    arrays = max(source[0] for source in sources) + 1
    middle_rows, end_rows = refs[:blocks], refs[blocks : 2 * blocks]
    refs = refs[2 * blocks :]
    pieces = refs[:arrays]
    cos_ref, sin_ref, gain_ref, out = refs[arrays : arrays + 4]
    taken, held, made, row_sems, sems, out_sems = refs[arrays + 4 :]
    depth = taken.shape[1] // 16
    columns = made.shape[1]
    steps = columns // tile

    def copies(step):
        listed = []
        for index, (array, first, group, slot) in enumerate(sources):
            start = pl.multiple_of((scal[group] * 4 + scal[slot]) * depth, 16)
            low = step * tile
            listed.append(
                pltpu.make_async_copy(
                    pieces[array].at[first : first + depth, low : low + tile],
                    held.at[step % 2, pl.ds(start, depth), :],
                    sems.at[step % 2, index],
                )
            )
        return listed

    starts = [sum(counts[:n]) for n in range(blocks)]
    row_copies = [
        [
            pltpu.make_async_copy(ref, taken.at[first : first + rows, :], row_sems.at[number])
            for ref in (middle_rows[number], end_rows[number])
        ]
        for number, (first, rows) in enumerate(zip(starts, counts))
    ]
    out_copies = []
    for copy in copies(0):
        copy.start()
    for in_middle, in_end in row_copies:
        pl.when(scal[8] == 1)(in_middle.start)
        pl.when(scal[8] == 0)(in_end.start)
    for step in range(steps):
        if step + 1 < steps:
            for copy in copies(step + 1):
                copy.start()
        if step == 0:
            for in_middle, _ in row_copies:
                in_middle.wait()
        for copy in copies(step):
            copy.wait()
        total = jnp.dot(taken[...], held[step % 2], preferred_element_type=jnp.float32)
        for number, (first, rows) in enumerate(zip(starts, counts)):
            place = pl.ds(pl.multiple_of(scal[9 + number], 16), rows)
            cosine = cos_ref[place, :]
            sine = sin_ref[place, :]
            for head in range(tile // HD):
                kind = (step * (tile // HD) + head) % (GQ + 2)
                vec = total[first : first + rows, head * HD : (head + 1) * HD]
                if kind <= GQ:
                    scale = lax.rsqrt(jnp.mean(vec * vec, axis=-1, keepdims=True) + 1e-06)
                    gain = gain_ref[0:1, :] if kind < GQ else gain_ref[1:2, :]
                    vec = vec * scale * gain
                    vec = vec * cosine + pltpu.roll(vec, HD // 2, 1) * sine
                at = step * tile + head * HD
                made[first : first + rows, at : at + HD] = vec.astype(made.dtype)
        at = slice(step * tile, (step + 1) * tile)
        out_copies.append(pltpu.make_async_copy(made.at[:, at], out.at[:, at], out_sems.at[step]))
        out_copies[-1].start()
    for copy in out_copies:
        copy.wait()


def project(rows_list, places, pieces, scal, cos, sin, gains, vmem_bytes):
    depth = rows_list[0][0].shape[1] // 16
    columns = pieces[0].shape[1]
    sources = [(n, m * depth, 4 + m, n) for n in range(4) for m in range(4)]
    counts = [r.shape[0] for r, _ in rows_list]
    steps = 3
    tile = columns // steps
    count = sum(counts)
    width = rows_list[0][0].shape[1]
    scal = jnp.concatenate([scal, jnp.stack(places)]).astype(jnp.int32)
    vmem = pl.BlockSpec(memory_space=pltpu.VMEM)
    hbm = pl.BlockSpec(memory_space=pltpu.HBM)
    return pl.pallas_call(
        functools.partial(project_kernel, counts, sources, tile),
        out_shape=pltpu.HBM((count, columns), jnp.bfloat16),
        in_specs=[pl.BlockSpec(memory_space=pltpu.SMEM)]
        + [hbm] * (2 * len(counts) + len(pieces))
        + [vmem] * 3,
        out_specs=hbm,
        scratch_shapes=[
            pltpu.VMEM((count, width), jnp.bfloat16),
            pltpu.VMEM((2, width, tile), jnp.bfloat16),
            pltpu.VMEM((count, columns), jnp.bfloat16),
            pltpu.SemaphoreType.DMA((len(counts),)),
            pltpu.SemaphoreType.DMA((2, 16)),
            pltpu.SemaphoreType.DMA((steps,)),
        ],
        compiler_params=pltpu.CompilerParams(vmem_limit_bytes=vmem_bytes),
        cost_estimate=pl.CostEstimate(
            flops=2 * count * width * columns,
            bytes_accessed=2 * (width * columns + count * (width + columns)),
            transcendentals=0,
        ),
        name="project",
    )(scal, *[r for r, _ in rows_list], *[r for _, r in rows_list], *pieces, cos, sin, gains)


FACTOR = LOG2E / float(HD) ** 0.5
CONTRACT = (((1,), (1,)), ((), ()))


def fetch_blocks(refs, parts, places, held, sems):
    copies = []
    for ref, blocks in zip(refs, parts):
        for first, rows, number in blocks:
            place = pl.ds(pl.multiple_of(places(number), 16), rows)
            copies.append(
                pltpu.make_async_copy(
                    ref.at[first : first + rows, :], held.at[place, :], sems.at[number]
                )
            )
    for copy in copies:
        copy.start()
    for copy in copies:
        copy.wait()


def head_columns(head):
    base = head // GQ * (GQ + 2) * HD
    query = base + head % GQ * HD
    key = base + GQ * HD
    return (
        slice(query, query + HD),
        slice(key, key + HD),
        slice(key + HD, key + 2 * HD),
        slice(head * HD, (head + 1) * HD),
    )


def attend_rows(held, head, low, block, length):
    query_at, key_at, value_at, _ = head_columns(head)
    high = low + block
    row = lax.broadcasted_iota(jnp.int32, (block, block), 0)
    col = lax.broadcasted_iota(jnp.int32, (block, block), 1)
    query = held[low:high, query_at]
    last = lax.dot_general(
        query, held[low:high, key_at], CONTRACT, preferred_element_type=jnp.float32
    )
    last = jnp.where((col <= row) & (col + low < length), last, -1e30)
    top = jnp.max(last, axis=-1, keepdims=True)
    if low:
        rest = lax.dot_general(
            query, held[:low, key_at], CONTRACT, preferred_element_type=jnp.float32
        )
        keys = lax.broadcasted_iota(jnp.int32, (1, low), 1)
        rest = rest + jnp.where(keys < length, 0.0, -1e30)
        top = jnp.maximum(top, jnp.max(rest, axis=-1, keepdims=True))
    probs = jnp.exp2((last - top) * FACTOR)
    norm = jnp.sum(probs, axis=-1, keepdims=True)
    value = jnp.dot(
        probs.astype(jnp.bfloat16), held[low:high, value_at], preferred_element_type=jnp.float32
    )
    if low:
        probs = jnp.exp2((rest - top) * FACTOR)
        norm = norm + jnp.sum(probs, axis=-1, keepdims=True)
        value = value + jnp.dot(
            probs.astype(jnp.bfloat16), held[:low, value_at], preferred_element_type=jnp.float32
        )
    return top, norm, value


def attend_near_kernel(parts, block, scal, *refs):
    partial, stats, held, sems = refs[len(parts) :]
    fetch_blocks(refs, parts, lambda number: scal[2 + number], held, sems)
    heads = partial.shape[1] // HD
    for head in range(heads):
        out_at = head_columns(head)[3]
        for low in range(0, held.shape[0], block):
            top, norm, value = attend_rows(held, head, low, block, scal[0])
            partial[low : low + block, out_at] = value / norm
            stats[low : low + block, head : head + 1] = top * FACTOR + jnp.log(norm) * LOG2E


def attend_far_kernel(parts, block, scal, *refs):
    partial, stats, out, held, sems = refs[len(parts) :]
    fetch_blocks(refs, parts, lambda number: scal[2 + number], held, sems)
    heads = out.shape[1] // HD
    total = held.shape[0]
    length = scal[0]

    @pl.when(scal[1] == 0)
    def _():
        low = total - block
        for head in range(heads):
            out_at = head_columns(head)[3]
            _, norm, value = attend_rows(held, head, low, block, length)
            out[low:, out_at] = (value / norm).astype(out.dtype)
        out[:low, :] = partial[...].astype(out.dtype)

    @pl.when(scal[1] == 1)
    def _():
        for head in range(heads):
            query_at, key_at, value_at, out_at = head_columns(head)
            _, norm, value = attend_rows(held, head, 0, block, length)
            out[:block, out_at] = (value / norm).astype(out.dtype)
            scores = lax.dot_general(
                held[block:, query_at],
                held[:block, key_at],
                CONTRACT,
                preferred_element_type=jnp.float32,
            )
            keys = lax.broadcasted_iota(jnp.int32, (1, block), 1)
            scores = scores * FACTOR + jnp.where(keys < length, 0.0, -1e30)
            before = stats[:, head : head + 1]
            top = jnp.maximum(before, jnp.max(scores, axis=-1, keepdims=True))
            probs = jnp.exp2(scores - top)
            scale = jnp.exp2(before - top)
            norm = scale + jnp.sum(probs, axis=-1, keepdims=True)
            value = partial[:, out_at] * scale + jnp.dot(
                probs.astype(jnp.bfloat16),
                held[:block, value_at],
                preferred_element_type=jnp.float32,
            )
            out[block:, out_at] = (value / norm).astype(out.dtype)


def attend_blocks(arrays, parts, places, length, side, block, partial=None):
    rows = sum(a.shape[0] for a in arrays)
    columns = arrays[0].shape[1]
    wide = columns // (GQ + 2) * GQ
    scal = jnp.stack([length, side] + list(places)).astype(jnp.int32)
    hbm = pl.BlockSpec(memory_space=pltpu.HBM)
    vmem = pl.BlockSpec(memory_space=pltpu.VMEM)
    if partial is None:
        body, name = attend_near_kernel, "attend_near"
        out_shape = [
            jax.ShapeDtypeStruct((rows, wide), jnp.float32),
            jax.ShapeDtypeStruct((rows, HD), jnp.float32),
        ]
    else:
        body, name = attend_far_kernel, "attend_far"
        out_shape = [jax.ShapeDtypeStruct((rows, wide), jnp.bfloat16)]
    extra = [] if partial is None else list(partial)
    return pl.pallas_call(
        functools.partial(body, parts, block),
        out_shape=out_shape,
        in_specs=[pl.BlockSpec(memory_space=pltpu.SMEM)]
        + [hbm] * len(arrays)
        + [vmem] * len(extra),
        out_specs=[vmem] * len(out_shape),
        scratch_shapes=[
            pltpu.VMEM((rows, columns), jnp.bfloat16),
            pltpu.SemaphoreType.DMA((len(places),)),
        ],
        compiler_params=pltpu.CompilerParams(vmem_limit_bytes=VMEM_BYTES // 2),
        cost_estimate=pl.CostEstimate(
            flops=2 * rows * rows * wide,
            bytes_accessed=2 * rows * (columns + wide),
            transcendentals=rows * rows * wide // HD // 2,
        ),
        name=name,
    )(scal, *arrays, *extra)


def after(x, *earlier):
    return lax.optimization_barrier((x,) + earlier)[0]


def four_planes(tokens, w_qkv, norm_gain, q_gain, k_gain, lengths):
    t = lax.axis_index("tensor")
    rows = tokens.shape[0]
    half = rows // 2
    columns = w_qkv.shape[1] // 4
    side = t // 2
    far_end = 3 * (1 - side)
    far_mid = 2 - side

    def slab(block):
        return lax.dynamic_slice(w_qkv, (0, block * columns), (w_qkv.shape[0], columns))

    def across(x, pairs):
        return lax.ppermute(x, "tensor", pairs)

    def exchange(x, bits):
        return across(x, [(i, i ^ bits) for i in range(4)])

    def spread(x):
        return lax.all_gather(x, "fsdp", axis=0, tiled=True)

    swap = [(1, 2), (2, 1)]
    far = [(0, 2), (3, 1)]
    outward = [(1, 0), (2, 3)]

    planes = [t] + [jnp.bitwise_xor(t, m) for m in (1, 2, 3)]
    own, out1, out2, out3 = [slab(p) for p in planes]
    normed = head_norm(tokens.astype(jnp.float32), norm_gain).astype(jnp.bfloat16)
    first, second = normed[:half], normed[half:]

    in2, in3, in1 = exchange(out2, 2), exchange(out3, 3), exchange(out1, 1)
    quarter = rows // 4
    pair1 = exchange(normed[:quarter], 1)
    second_pair, third_pair = normed[quarter : quarter + half], normed[quarter + half :]
    in1, in2, in3, pair1, first, second, second_pair, third_pair = lax.optimization_barrier(
        (in1, in2, in3, pair1, first, second, second_pair, third_pair)
    )
    swap1 = across(first, swap)
    pair2 = exchange(second_pair, 1)
    swap2 = across(after(second, swap1, pair2), swap)
    pair3 = exchange(after(third_pair, pair2), 1)
    on1 = across(swap1, outward)
    far1 = across(after(first, swap2, pair3), far)
    on2 = across(swap2, outward)
    far2 = across(after(second, far1, on1), far)
    on3 = across(far1, outward)

    pieces = [spread(x) for x in (own, in1, in2, in3)]
    middle = jnp.where((t == 1) | (t == 2), 1, 0)
    scal = jnp.stack(planes + [jnp.int32(m) for m in range(4)] + [middle])

    positions = jnp.arange(4 * rows, dtype=jnp.int32)
    angle = angles(positions)
    cos = jnp.concatenate([jnp.cos(angle)] * 2, axis=1)
    sin = jnp.concatenate([-jnp.sin(angle), jnp.sin(angle)], axis=1)
    gains = jnp.stack([q_gain, k_gain])

    made, parts, places = [], [], []

    tables = (cos, sin, gains)

    def run(call, vmem_bytes=VMEM_BYTES):
        listed, first_row = [], 0
        for (block, _), place in call:
            listed.append((first_row, block.shape[0], len(places)))
            first_row += block.shape[0]
            places.append(place)
        parts.append(listed)
        made.append(
            project([b for b, _ in call], [p for _, p in call], pieces, scal, *tables, vmem_bytes)
        )

    pair_place = planes[1] * rows
    run(
        [
            ((normed, normed), t * rows),
            ((pair1, pair1), pair_place),
            ((pair2, pair2), pair_place + quarter),
            ((pair3, pair3), pair_place + quarter + half),
        ]
    )
    on4 = across(after(far2, on2, made[0]), outward)
    run([((swap1, on1), far_mid * rows), ((swap2, on2), far_mid * rows + half)])
    near_places = [place - side * rows for place in places]
    made[1] = after(made[1], on3)
    partial = attend_blocks(made, parts, near_places, lengths[0] - side * rows, side, rows)
    far1, on3, far2, on4 = [after(x, *partial) for x in (far1, on3, far2, on4)]
    run([((far1, on3), far_end * rows), ((far2, on4), far_end * rows + half)], VMEM_BYTES // 2)
    return attend_blocks(made, parts, places, lengths[0], side, rows, partial)[0]


def solution(mesh):
    placed = (
        P(("groups", "fsdp", "tensor"), None),
        P(("groups", "fsdp", "tensor"), None),
        P(),
        P(),
        P(),
        P(("groups", "fsdp")),
    )
    sizes = dict(mesh.shape)
    body = four_planes if sizes["tensor"] == 4 and sizes["fsdp"] == 4 else any_mesh
    return jax.shard_map(
        body,
        mesh=mesh,
        in_specs=placed,
        out_specs=P(("groups", "fsdp"), "tensor"),
        check_vma=False,
    )
```

profile of v0, /device:TPU:24, one launch (start us, length us, event | category | flops | bytes accessed | tf_op | source)
XLA Modules:
  0.0 295.8 jit_solution(3326867345027677893)
XLA Ops:
  6.5 4.3 %constant_dynamic-slice_fusion = (bf16[320,1536]{1,0:T(8,128)(2,1)}, bf16[320,1536]{1,0:T(8,128)(2,1)}, bf16[320,1536]{1,0:T(8,128)(2,1)}, bf16[320,1536]{1,0:T(8,128)(2,1)}) fusion(bf16[320,6144]{1,0:T(8,128)(2,1)} %param.7, s32[]{:T(128)S(6)} %select_n.26, s32[]{:T(128)S(6)} %select_n.24, s32[]{:T(128)S(6)} %select_n.23, s32[]{:T(128)S(6)} %select_n.25), kind=kLoop, calls=%fused_computation.13 | loop fusion | bytes 7864336 | tf_op jit(solution)/shard_map/dynamic_slice | solution.py:353
  10.8 0.0 all-gather.7.cloned.1.call-start
  10.9 0.6 fusion
  11.5 0.0 copy-done.21
  11.5 0.8 fusion.2.refs_0_.refs_4_
  12.3 0.9 fusion.4
  13.2 0.4 collective-permute-start.3
  13.7 0.5 copy-done.20
  14.2 0.3 collective-permute-start.1
  14.6 1.0 collective-permute-start
  15.6 3.0 %collective-permute-start.2 = (bf16[320,1536]{1,0:T(8,128)(2,1)}, bf16[320,1536]{1,0:T(8,128)(2,1)}, u32[]{:S(2)}, u32[]{:S(2)}) collective-permute-start(bf16[320,1536]{1,0:T(8,128)(2,1)} %get-tuple-element.48), channel_id=1, source_target_pairs={{0,3},{1,2},{2,1},{3,0},{4,7},{5,6},{6,5},{7,4},{8,11},{9,10},{10,... | collective-permute-start | bytes 2949128 | tf_op jit(solution)/shard_map/ppermute | solution.py:356
  18.6 1.5 fusion.5
  20.2 22.6 %collective-permute-done.3.refs_1_.refs_5_ = bf16[64,5120]{1,0:T(8,128)(2,1)S(1)} collective-permute-done((bf16[64,5120]{1,0:T(8,128)(2,1)S(1)}, bf16[64,5120]{1,0:T(8,128)(2,1)S(1)}, u32[]{:S(2)}, u32[]{:S(2)}) %collective-permute-start.3) | collective-permute-done | bytes 655392 | tf_op jit(solution)/shard_map/ppermute | solution.py:356
  42.8 18.2 %collective-permute-done.1 = bf16[320,1536]{1,0:T(8,128)(2,1)} collective-permute-done((bf16[320,1536]{1,0:T(8,128)(2,1)S(1)}, bf16[320,1536]{1,0:T(8,128)(2,1)}, u32[]{:S(2)}, u32[]{:S(2)}) %collective-permute-start.1) | collective-permute-done | bytes 983072 | tf_op jit(solution)/shard_map/ppermute | solution.py:356
  61.0 32.0 %collective-permute-done = bf16[320,1536]{1,0:T(8,128)(2,1)} collective-permute-done((bf16[320,1536]{1,0:T(8,128)(2,1)}, bf16[320,1536]{1,0:T(8,128)(2,1)}, u32[]{:S(2)}, u32[]{:S(2)}) %collective-permute-start) | collective-permute-done | bytes 983072 | tf_op jit(solution)/shard_map/ppermute | solution.py:356
  93.0 0.0 all-gather.7.cloned.1.call-update
  93.1 0.0 all-gather.9.cloned.1.call-start
  93.1 0.7 all-gather.9.cloned.1.call-update
  93.8 0.0 all-gather.11.cloned.1.call-start
  93.8 0.5 all-gather.11.cloned.1.call-update
  94.4 9.6 %collective-permute-start.4 = (bf16[128,5120]{1,0:T(8,128)(2,1)S(1)}, bf16[128,5120]{1,0:T(8,128)(2,1)S(1)}, u32[]{:S(2)}, u32[]{:S(2)}) collective-permute-start(bf16[128,5120]{1,0:T(8,128)(2,1)S(1)} %get-tuple-element.26), channel_id=1, source_target_pairs={{0,1},{1,0},{2,3},{3,2},{4,5},{5,4},{6,7},{7,6},{8,9},{9,8},{10,11... | collective-permute-start | bytes 3932168 | tf_op jit(solution)/shard_map/ppermute | solution.py:356
  104.0 0.7 collective-permute-start.6
  104.7 27.2 %collective-permute-done.4.refs_2_.refs_6_ = bf16[128,5120]{1,0:T(8,128)(2,1)S(1)} collective-permute-done((bf16[128,5120]{1,0:T(8,128)(2,1)S(1)}, bf16[128,5120]{1,0:T(8,128)(2,1)S(1)}, u32[]{:S(2)}, u32[]{:S(2)}) %collective-permute-start.4) | collective-permute-done | bytes 1310752 | tf_op jit(solution)/shard_map/ppermute | solution.py:356
  132.0 1.1 copy-done.13
  133.0 0.7 collective-permute-start.7
  133.8 4.1 %collective-permute-start.5 = (bf16[64,5120]{1,0:T(8,128)(2,1)}, bf16[64,5120]{1,0:T(8,128)(2,1)S(1)}, u32[]{:S(2)}, u32[]{:S(2)}) collective-permute-start(bf16[64,5120]{1,0:T(8,128)(2,1)} %get-tuple-element.28), channel_id=1, source_target_pairs={{0,1},{1,0},{2,3},{3,2},{4,5},{5,4},{6,7},{7,6},{8,9},{9,8},{10,11... | collective-permute-start | bytes 1966088 | tf_op jit(solution)/shard_map/ppermute | solution.py:356
  137.9 1.3 collective-permute-start.8
  139.2 1.1 copy-done.7
  140.2 13.5 %collective-permute-done.5.refs_3_.refs_7_ = bf16[64,5120]{1,0:T(8,128)(2,1)S(1)} collective-permute-done((bf16[64,5120]{1,0:T(8,128)(2,1)}, bf16[64,5120]{1,0:T(8,128)(2,1)S(1)}, u32[]{:S(2)}, u32[]{:S(2)}) %collective-permute-start.5) | collective-permute-done | bytes 655392 | tf_op jit(solution)/shard_map/ppermute | solution.py:356
  153.7 0.8 copy-done.15
  154.6 15.0 %collective-permute-start.10 = (bf16[128,5120]{1,0:T(8,128)(2,1)}, bf16[128,5120]{1,0:T(8,128)(2,1)}, u32[]{:S(2)}, u32[]{:S(2)}) collective-permute-start(bf16[128,5120]{1,0:T(8,128)(2,1)} %copy-done.19), channel_id=1, source_target_pairs={{0,2},{3,1},{4,6},{7,5},{8,10},{11,9},{12,14},{15,13},{16,18},{19,... | collective-permute-start | bytes 3932168 | tf_op jit(solution)/shard_map/ppermute | solution.py:356
  169.6 1.3 collective-permute-start.9
  170.9 10.9 %collective-permute-done.8.refs_2_ = bf16[128,5120]{1,0:T(8,128)(2,1)S(1)} collective-permute-done((bf16[128,5120]{1,0:T(8,128)(2,1)S(1)}, bf16[128,5120]{1,0:T(8,128)(2,1)S(1)}, u32[]{:S(2)}, u32[]{:S(2)}) %collective-permute-start.8) | collective-permute-done | bytes 1310752 | tf_op jit(solution)/shard_map/ppermute | solution.py:356
  181.8 1.0 copy-done.11
  182.9 11.8 %collective-permute-done.10.refs_0_ = bf16[128,5120]{1,0:T(8,128)(2,1)} collective-permute-done((bf16[128,5120]{1,0:T(8,128)(2,1)}, bf16[128,5120]{1,0:T(8,128)(2,1)}, u32[]{:S(2)}, u32[]{:S(2)}) %collective-permute-start.10) | collective-permute-done | bytes 1310752 | tf_op jit(solution)/shard_map/ppermute | solution.py:356
  194.6 6.4 %collective-permute-start.12 = (bf16[128,5120]{1,0:T(8,128)(2,1)}, bf16[128,5120]{1,0:T(8,128)(2,1)}, u32[]{:S(2)}, u32[]{:S(2)}) collective-permute-start(bf16[128,5120]{1,0:T(8,128)(2,1)} %get-tuple-element.40), channel_id=1, source_target_pairs={{0,2},{3,1},{4,6},{7,5},{8,10},{11,9},{12,14},{15,13},{16,18},{19,... | collective-permute-start | bytes 3932168 | tf_op jit(solution)/shard_map/ppermute | solution.py:356
  201.0 0.1 concatenate.18.scal
  201.1 1.9 fusion.3
  203.0 0.3 pad_maximum_fusion
  203.3 1.3 collective-permute-start.11
  204.6 0.0 all-gather.5.cloned.1.call-done.refs_8_.refs_4_
  204.7 0.0 all-gather.7.cloned.1.call-done.refs_9_.refs_5_
  204.7 0.0 all-gather.9.cloned.1.call-done.refs_10_.refs_6_
  204.7 0.0 all-gather.11.cloned.1.call-done.refs_11_.refs_7_
  204.8 1.3 copy-done.14
  206.1 1.1 copy-done.16
  207.2 16.5 %project.3.refs_0_ = bf16[512,1536]{1,0:T(8,128)(2,1)} custom-call(s32[13]{0:T(128)S(1)} %concatenate.18.scal, bf16[256,5120]{1,0:T(8,128)(2,1)} %copy-done.17, bf16[64,5120]{1,0:T(8,128)(2,1)S(1)} %collective-permute-done.3.refs_1_.refs_5_, bf16[128,5120]{1,0:T(8,128)(2,1)S(1)} %copy-done.14, bf16[64,5120]{1,0:T(8,128)(2,1)S(1)} %copy-done.16, ...), custom_call_target="tpu_custom_call" | custom-call | flops 8053063680 | bytes 22544384 | tf_op jit(solution)/shard_map/project/pallas_call | solution.py:157
  223.6 1.5 collective-permute-done.12.refs_1_
  225.1 1.3 collective-permute-start.13
  227.1 0.1 concatenate.22.scal
  227.2 0.1 concatenate.21.scal
  227.3 0.1 stack.97.scal
  227.4 0.1 stack.113.scal
  227.4 1.3 copy-done.8
  228.8 1.3 copy-done.10
  230.1 1.3 copy-done.12
  231.4 12.1 %project.4.refs_1_ = bf16[256,1536]{1,0:T(8,128)(2,1)} custom-call(s32[11]{0:T(128)S(1)} %concatenate.21.scal, bf16[128,5120]{1,0:T(8,128)(2,1)S(1)} %copy-done.8, bf16[128,5120]{1,0:T(8,128)(2,1)S(1)} %copy-done.10, bf16[128,5120]{1,0:T(8,128)(2,1)S(1)} %copy-done.12, bf16[128,5120]{1,0:T(8,128)(2,1)} %collective-permute-done.9.refs_3_, ...), custom_call_target="tpu_custom_call" | custom-call | flops 4026531840 | bytes 19136512 | tf_op jit(solution)/shard_map/project/pallas_call | solution.py:157
  243.5 1.3 copy-done.4
  244.8 10.2 %attend_near.1 = (f32[768,1024]{1,0:T(8,128)S(1)}, f32[768,128]{1,0:T(8,128)S(1)}) custom-call(s32[8]{0:T(128)S(1)} %stack.113.scal, bf16[512,1536]{1,0:T(8,128)(2,1)S(1)} %copy-done.6, bf16[256,1536]{1,0:T(8,128)(2,1)S(1)} %copy-done.4), custom_call_target="tpu_custom_call" | custom-call | flops 1207959552 | bytes 3932160 | tf_op jit(solution)/shard_map/attend_near/pallas_call | solution.py:318
  255.0 8.6 %collective-permute-done.13.refs_3_ = bf16[128,5120]{1,0:T(8,128)(2,1)} collective-permute-done((bf16[128,5120]{1,0:T(8,128)(2,1)}, bf16[128,5120]{1,0:T(8,128)(2,1)}, u32[]{:S(2)}, u32[]{:S(2)}) %collective-permute-start.13) | collective-permute-done | bytes 1310752 | tf_op jit(solution)/shard_map/ppermute | solution.py:356
  263.6 2.1 copy-done.3
  265.7 9.7 %project.5.refs_2_ = bf16[256,1536]{1,0:T(8,128)(2,1)} custom-call(s32[11]{0:T(128)S(1)} %concatenate.22.scal, bf16[128,5120]{1,0:T(8,128)(2,1)} %collective-permute-done.10.refs_0_, bf16[128,5120]{1,0:T(8,128)(2,1)} %collective-permute-done.12.refs_1_, bf16[128,5120]{1,0:T(8,128)(2,1)} %collective-permute-done.11.refs_2_, ...), custom_call_target="tpu_custom_call" | custom-call | flops 4026531840 | bytes 19136512 | tf_op jit(solution)/shard_map/project/pallas_call | solution.py:157
  275.4 1.1 copy-done.5
  276.6 12.3 %attend_far.1 = bf16[1024,1024]{1,0:T(8,128)(2,1)} custom-call(s32[10]{0:T(128)S(1)} %stack.97.scal, bf16[512,1536]{1,0:T(8,128)(2,1)S(1)} %copy-done.6, bf16[256,1536]{1,0:T(8,128)(2,1)S(1)} %copy-done.4, bf16[256,1536]{1,0:T(8,128)(2,1)S(1)} %copy-done.5, f32[768,1024]{1,0:T(8,128)S(1)} %get-tuple-element.37.refs_3_, f32[768,128]{1,0:T(8,128)S(1)} %get-tuple-element.38.refs_4_), custom_call_target="tpu_custom_call" | custom-call | flops 2147483648 | bytes 5242880 | tf_op jit(solution)/shard_map/attend_far/pallas_call | solution.py:318
  (45 shorter events, 0.1 us)
Async XLA Ops:
  6.5 198.1 %all-gather.5.cloned.1.call-start = ((), (), s32[]{:S(2)}) async-start(), calls=%async_computation | async-start | bytes 4915200 | tf_op jit(solution)/shard_map/all_gather | solution.py:362
  6.5 4.3 %copy-start.18 = (bf16[256,5120]{1,0:T(8,128)(2,1)S(1)}, bf16[256,5120]{1,0:T(8,128)(2,1)}, u32[]{:S(2)}) copy-start(bf16[256,5120]{1,0:T(8,128)(2,1)} %param.6) | copy-start | bytes 7864324
  10.8 0.7 copy-start.21
  10.8 193.9 %all-gather.7.cloned.1.call-start = ((), (), s32[]{:S(2)}) async-start(), calls=%async_computation.1 | async-start | bytes 4915200 | tf_op jit(solution)/shard_map/all_gather | solution.py:362
  12.3 7.9 %copy-start.17 = (bf16[256,5120]{1,0:T(8,128)(2,1)}, bf16[256,5120]{1,0:T(8,128)(2,1)S(1)}, u32[]{:S(2)}) copy-start(bf16[256,5120]{1,0:T(8,128)(2,1)S(1)} %fusion.2.refs_0_.refs_4_) | copy-start | bytes 7864324
  12.3 1.9 copy-start.20
  13.2 29.6 %collective-permute-start.3 = (bf16[64,5120]{1,0:T(8,128)(2,1)S(1)}, bf16[64,5120]{1,0:T(8,128)(2,1)S(1)}, u32[]{:S(2)}, u32[]{:S(2)}) collective-permute-start(bf16[64,5120]{1,0:T(8,128)(2,1)S(1)} %get-tuple-element.50), channel_id=1, source_target_pairs={{0,1},{1,0},{2,3},{3,2},{4,5},{5,4},{6,7},{7,6},{8,9},{9,8},{10,11... | collective-permute-start | bytes 1966088 | tf_op jit(solution)/shard_map/ppermute | solution.py:356
  14.2 46.8 %collective-permute-start.1 = (bf16[320,1536]{1,0:T(8,128)(2,1)S(1)}, bf16[320,1536]{1,0:T(8,128)(2,1)}, u32[]{:S(2)}, u32[]{:S(2)}) collective-permute-start(bf16[320,1536]{1,0:T(8,128)(2,1)S(1)} %copy-done.20), channel_id=1, source_target_pairs={{0,2},{1,3},{2,0},{3,1},{4,6},{5,7},{6,4},{7,5},{8,10},{9,11},{10,... | collective-permute-start | bytes 2949128 | tf_op jit(solution)/shard_map/ppermute | solution.py:356
  14.6 78.4 %collective-permute-start = (bf16[320,1536]{1,0:T(8,128)(2,1)}, bf16[320,1536]{1,0:T(8,128)(2,1)}, u32[]{:S(2)}, u32[]{:S(2)}) collective-permute-start(bf16[320,1536]{1,0:T(8,128)(2,1)} %get-tuple-element.47), channel_id=1, source_target_pairs={{0,1},{1,0},{2,3},{3,2},{4,5},{5,4},{6,7},{7,6},{8,9},{9,8},{10,11... | collective-permute-start | bytes 2949128 | tf_op jit(solution)/shard_map/ppermute | solution.py:356
  15.6 77.4 %collective-permute-start.2 = (bf16[320,1536]{1,0:T(8,128)(2,1)}, bf16[320,1536]{1,0:T(8,128)(2,1)}, u32[]{:S(2)}, u32[]{:S(2)}) collective-permute-start(bf16[320,1536]{1,0:T(8,128)(2,1)} %get-tuple-element.48), channel_id=1, source_target_pairs={{0,3},{1,2},{2,1},{3,0},{4,7},{5,6},{6,5},{7,4},{8,11},{9,10},{10,... | collective-permute-start | bytes 2949128 | tf_op jit(solution)/shard_map/ppermute | solution.py:356
  20.2 111.8 %copy-start.19 = (bf16[128,5120]{1,0:T(8,128)(2,1)}, bf16[128,5120]{1,0:T(8,128)(2,1)S(1)}, u32[]{:S(2)}) copy-start(bf16[128,5120]{1,0:T(8,128)(2,1)S(1)} %get-tuple-element.35) | copy-start | bytes 3932164
  20.2 149.4 %copy-start.22 = (f32[128]{0:T(128)S(1)}, f32[128]{0:T(128)}, u32[]{:S(2)}) copy-start(f32[128]{0:T(128)} %param.10) | copy-start | bytes 1540
  20.2 149.4 %copy-start.23 = (f32[128]{0:T(128)S(1)}, f32[128]{0:T(128)}, u32[]{:S(2)}) copy-start(f32[128]{0:T(128)} %param.9) | copy-start | bytes 1540
  93.1 111.7 %all-gather.9.cloned.1.call-start = ((), (), s32[]{:S(2)}) async-start(), calls=%async_computation.2 | async-start | bytes 4915200 | tf_op jit(solution)/shard_map/all_gather | solution.py:362
  93.8 110.9 %all-gather.11.cloned.1.call-start = ((), (), s32[]{:S(2)}) async-start(), calls=%async_computation.3 | async-start | bytes 4915200 | tf_op jit(solution)/shard_map/all_gather | solution.py:362
  94.4 37.6 %collective-permute-start.4 = (bf16[128,5120]{1,0:T(8,128)(2,1)S(1)}, bf16[128,5120]{1,0:T(8,128)(2,1)S(1)}, u32[]{:S(2)}, u32[]{:S(2)}) collective-permute-start(bf16[128,5120]{1,0:T(8,128)(2,1)S(1)} %get-tuple-element.26), channel_id=1, source_target_pairs={{0,1},{1,0},{2,3},{3,2},{4,5},{5,4},{6,7},{7,6},{8,9},{9,8},{10,11... | collective-permute-start | bytes 3932168 | tf_op jit(solution)/shard_map/ppermute | solution.py:356
  104.0 29.0 %collective-permute-start.6 = (bf16[128,5120]{1,0:T(8,128)(2,1)S(1)}, bf16[128,5120]{1,0:T(8,128)(2,1)S(1)}, u32[]{:S(2)}, u32[]{:S(2)}) collective-permute-start(bf16[128,5120]{1,0:T(8,128)(2,1)S(1)} %get-tuple-element.35), channel_id=1, source_target_pairs={{1,2},{2,1},{5,6},{6,5},{9,10},{10,9},{13,14},{14,13},{17,18},{18,... | collective-permute-start | bytes 3932168 | tf_op jit(solution)/shard_map/ppermute | solution.py:356
  131.9 1.1 copy-start.13
  133.0 21.6 %collective-permute-start.7 = (bf16[128,5120]{1,0:T(8,128)(2,1)}, bf16[128,5120]{1,0:T(8,128)(2,1)S(1)}, u32[]{:S(2)}, u32[]{:S(2)}) collective-permute-start(bf16[128,5120]{1,0:T(8,128)(2,1)} %get-tuple-element.40), channel_id=1, source_target_pairs={{1,2},{2,1},{5,6},{6,5},{9,10},{10,9},{13,14},{14,13},{17,18},{18,... | collective-permute-start | bytes 3932168 | tf_op jit(solution)/shard_map/ppermute | solution.py:356
  133.8 20.0 %collective-permute-start.5 = (bf16[64,5120]{1,0:T(8,128)(2,1)}, bf16[64,5120]{1,0:T(8,128)(2,1)S(1)}, u32[]{:S(2)}, u32[]{:S(2)}) collective-permute-start(bf16[64,5120]{1,0:T(8,128)(2,1)} %get-tuple-element.28), channel_id=1, source_target_pairs={{0,1},{1,0},{2,3},{3,2},{4,5},{5,4},{6,7},{7,6},{8,9},{9,8},{10,11... | collective-permute-start | bytes 1966088 | tf_op jit(solution)/shard_map/ppermute | solution.py:356
  137.9 43.9 %collective-permute-start.8 = (bf16[128,5120]{1,0:T(8,128)(2,1)S(1)}, bf16[128,5120]{1,0:T(8,128)(2,1)S(1)}, u32[]{:S(2)}, u32[]{:S(2)}) collective-permute-start(bf16[128,5120]{1,0:T(8,128)(2,1)S(1)} %collective-permute-done.6.refs_0_), channel_id=1, source_target_pairs={{1,0},{2,3},{5,4},{6,7},{9,8},{10,11},{13,12},{14,15},{17,16},{18,... | collective-permute-start | bytes 3932168 | tf_op jit(solution)/shard_map/ppermute | solution.py:356
  139.1 1.1 copy-start.7
  153.7 0.8 copy-start.15
  154.6 69.1 %copy-start.9 = (bf16[128,5120]{1,0:T(8,128)(2,1)}, bf16[128,5120]{1,0:T(8,128)(2,1)S(1)}, u32[]{:S(2)}) copy-start(bf16[128,5120]{1,0:T(8,128)(2,1)S(1)} %collective-permute-done.7.refs_1_) | copy-start | bytes 3932164
  154.6 40.1 %collective-permute-start.10 = (bf16[128,5120]{1,0:T(8,128)(2,1)}, bf16[128,5120]{1,0:T(8,128)(2,1)}, u32[]{:S(2)}, u32[]{:S(2)}) collective-permute-start(bf16[128,5120]{1,0:T(8,128)(2,1)} %copy-done.19), channel_id=1, source_target_pairs={{0,2},{3,1},{4,6},{7,5},{8,10},{11,9},{12,14},{15,13},{16,18},{19,... | collective-permute-start | bytes 3932168 | tf_op jit(solution)/shard_map/ppermute | solution.py:356
  169.6 54.0 %collective-permute-start.9 = (bf16[128,5120]{1,0:T(8,128)(2,1)S(1)}, bf16[128,5120]{1,0:T(8,128)(2,1)}, u32[]{:S(2)}, u32[]{:S(2)}) collective-permute-start(bf16[128,5120]{1,0:T(8,128)(2,1)S(1)} %collective-permute-done.7.refs_1_), channel_id=1, source_target_pairs={{1,0},{2,3},{5,4},{6,7},{9,8},{10,11},{13,12},{14,15},{17,16},{18,... | collective-permute-start | bytes 3932168 | tf_op jit(solution)/shard_map/ppermute | solution.py:356
  181.8 1.1 copy-start.11
  194.6 30.5 %collective-permute-start.12 = (bf16[128,5120]{1,0:T(8,128)(2,1)}, bf16[128,5120]{1,0:T(8,128)(2,1)}, u32[]{:S(2)}, u32[]{:S(2)}) collective-permute-start(bf16[128,5120]{1,0:T(8,128)(2,1)} %get-tuple-element.40), channel_id=1, source_target_pairs={{0,2},{3,1},{4,6},{7,5},{8,10},{11,9},{12,14},{15,13},{16,18},{19,... | collective-permute-start | bytes 3932168 | tf_op jit(solution)/shard_map/ppermute | solution.py:356
  203.3 40.2 %collective-permute-start.11 = (bf16[128,5120]{1,0:T(8,128)(2,1)}, bf16[128,5120]{1,0:T(8,128)(2,1)}, u32[]{:S(2)}, u32[]{:S(2)}) collective-permute-start(bf16[128,5120]{1,0:T(8,128)(2,1)} %collective-permute-done.10.refs_0_), channel_id=1, source_target_pairs={{1,0},{2,3},{5,4},{6,7},{9,8},{10,11},{13,12},{14,15},{17,16},{18,... | collective-permute-start | bytes 3932168 | tf_op jit(solution)/shard_map/ppermute | solution.py:356
  204.7 1.3 copy-start.14
  206.1 1.1 copy-start.16
  225.1 38.5 %collective-permute-start.13 = (bf16[128,5120]{1,0:T(8,128)(2,1)}, bf16[128,5120]{1,0:T(8,128)(2,1)}, u32[]{:S(2)}, u32[]{:S(2)}) collective-permute-start(bf16[128,5120]{1,0:T(8,128)(2,1)} %collective-permute-done.12.refs_1_), channel_id=1, source_target_pairs={{1,0},{2,3},{5,4},{6,7},{9,8},{10,11},{13,12},{14,15},{17,16},{18,... | collective-permute-start | bytes 3932168 | tf_op jit(solution)/shard_map/ppermute | solution.py:356
  227.4 1.3 copy-start.8
  228.8 1.3 copy-start.10
  230.1 1.3 copy-start.12
  231.4 12.1 %copy-start.6 = (bf16[512,1536]{1,0:T(8,128)(2,1)S(1)}, bf16[512,1536]{1,0:T(8,128)(2,1)}, u32[]{:S(2)}) copy-start(bf16[512,1536]{1,0:T(8,128)(2,1)} %project.3.refs_0_) | copy-start | bytes 4718596
  231.4 32.2 %copy-start.1 = (bf16[1280,1536]{1,0:T(8,128)(2,1)S(1)}, bf16[1280,1536]{1,0:T(8,128)(2,1)}, u32[]{:S(2)}) copy-start(bf16[1280,1536]{1,0:T(8,128)(2,1)} %all-gather.7.cloned.1.call-done.refs_9_.refs_5_) | copy-start | bytes 11796484
  231.4 32.2 %copy-start.2 = (bf16[1280,1536]{1,0:T(8,128)(2,1)S(1)}, bf16[1280,1536]{1,0:T(8,128)(2,1)}, u32[]{:S(2)}) copy-start(bf16[1280,1536]{1,0:T(8,128)(2,1)} %all-gather.9.cloned.1.call-done.refs_10_.refs_6_) | copy-start | bytes 11796484
  243.5 20.1 %copy-start = (bf16[1280,1536]{1,0:T(8,128)(2,1)S(1)}, bf16[1280,1536]{1,0:T(8,128)(2,1)}, u32[]{:S(2)}) copy-start(bf16[1280,1536]{1,0:T(8,128)(2,1)} %all-gather.5.cloned.1.call-done.refs_8_.refs_4_) | copy-start | bytes 11796484
  243.5 1.3 copy-start.4
  263.6 2.1 copy-start.3
  275.4 1.1 copy-start.5
Sparse Core Ops, SparseCore 0:
  10.9 33.9 all-gather.4
  93.2 42.0 all-gather.6
  136.9 33.0 all-gather.8
  171.4 32.9 all-gather.10
where the time goes:
time: 301 us; the launch traced here: 296 us
  waiting for transfers between devices  148 us (49%)
  Pallas kernels  60.6 us (20%)
  starting transfers between devices  46.7 us (16%)
  local copies, waits for them, and re-layouts  22.7 us (8%)
  between operations  14.5 us (5%)
  other arithmetic  3.63 us (1%)
    ppermute x14, waiting for transfers between devices, across(): return lax.ppermute(x, 'tensor', pairs)  146 us
    ppermute x14, starting transfers between devices, across(): return lax.ppermute(x, 'tensor', pairs)  46.5 us
    pallas_call x3, Pallas kernels, project(): pl.pallas_call(functools.partial(project_kernel, counts, sources, tile),...  38.2 us
    pallas_call x2, Pallas kernels, attend_blocks(): pl.pallas_call(functools.partial(body, parts, block), out_shape=out_shape...  22.4 us
    unnamed x48, local copies, waits for them, and re-layouts  15.5 us
  transfers between devices with their start and end apart: 18, of which 9 were waited for; matrix products, arithmetic and copies ran while one was open for 2% of the time, Pallas kernels for 13%

commit v1 on v0

--- a/solution.py
+++ b/solution.py
@@ -11,6 +11,7 @@
 GQ = 4
 LOG2E = 1.4426950408889634
 VMEM_BYTES = 48 * 1024 * 1024
+SMALL_BYTES = 20 * 1024 * 1024
 
 
 def head_norm(vec, gain):
@@ -142,7 +143,7 @@
         copy.wait()
 
 
-def project(rows_list, places, pieces, scal, cos, sin, gains, vmem_bytes):
+def project(rows_list, places, pieces, scal, cos, sin, gains, vmem_bytes, space):
     depth = rows_list[0][0].shape[1] // 16
     columns = pieces[0].shape[1]
     sources = [(n, m * depth, 4 + m, n) for n in range(4) for m in range(4)]
@@ -156,11 +157,11 @@
     hbm = pl.BlockSpec(memory_space=pltpu.HBM)
     return pl.pallas_call(
         functools.partial(project_kernel, counts, sources, tile),
-        out_shape=pltpu.HBM((count, columns), jnp.bfloat16),
+        out_shape=space((count, columns), jnp.bfloat16),
         in_specs=[pl.BlockSpec(memory_space=pltpu.SMEM)]
         + [hbm] * (2 * len(counts) + len(pieces))
         + [vmem] * 3,
-        out_specs=hbm,
+        out_specs=pl.BlockSpec(memory_space=space),
         scratch_shapes=[
             pltpu.VMEM((count, width), jnp.bfloat16),
             pltpu.VMEM((2, width, tile), jnp.bfloat16),
@@ -326,7 +327,7 @@
             pltpu.VMEM((rows, columns), jnp.bfloat16),
             pltpu.SemaphoreType.DMA((len(places),)),
         ],
-        compiler_params=pltpu.CompilerParams(vmem_limit_bytes=VMEM_BYTES // 2),
+        compiler_params=pltpu.CompilerParams(vmem_limit_bytes=SMALL_BYTES),
         cost_estimate=pl.CostEstimate(
             flops=2 * rows * rows * wide,
             bytes_accessed=2 * rows * (columns + wide),
@@ -371,11 +372,17 @@
     first, second = normed[:half], normed[half:]
 
     in2, in3, in1 = exchange(out2, 2), exchange(out3, 3), exchange(out1, 1)
+    positions = jnp.arange(4 * rows, dtype=jnp.int32)
+    angle = angles(positions)
+    cos = jnp.concatenate([jnp.cos(angle)] * 2, axis=1)
+    sin = jnp.concatenate([-jnp.sin(angle), jnp.sin(angle)], axis=1)
     quarter = rows // 4
     pair1 = exchange(normed[:quarter], 1)
     second_pair, third_pair = normed[quarter : quarter + half], normed[quarter + half :]
-    in1, in2, in3, pair1, first, second, second_pair, third_pair = lax.optimization_barrier(
-        (in1, in2, in3, pair1, first, second, second_pair, third_pair)
+    in1, in2, in3, pair1, first, second, second_pair, third_pair, cos, sin = (
+        lax.optimization_barrier(
+            (in1, in2, in3, pair1, first, second, second_pair, third_pair, cos, sin)
+        )
     )
     swap1 = across(first, swap)
     pair2 = exchange(second_pair, 1)
@@ -391,17 +398,13 @@
     middle = jnp.where((t == 1) | (t == 2), 1, 0)
     scal = jnp.stack(planes + [jnp.int32(m) for m in range(4)] + [middle])
 
-    positions = jnp.arange(4 * rows, dtype=jnp.int32)
-    angle = angles(positions)
-    cos = jnp.concatenate([jnp.cos(angle)] * 2, axis=1)
-    sin = jnp.concatenate([-jnp.sin(angle), jnp.sin(angle)], axis=1)
     gains = jnp.stack([q_gain, k_gain])
 
     made, parts, places = [], [], []
 
     tables = (cos, sin, gains)
 
-    def run(call, vmem_bytes=VMEM_BYTES):
+    def run(call, vmem_bytes=VMEM_BYTES, space=pltpu.HBM):
         listed, first_row = [], 0
         for (block, _), place in call:
             listed.append((first_row, block.shape[0], len(places)))
@@ -409,7 +412,7 @@
             places.append(place)
         parts.append(listed)
         made.append(
-            project([b for b, _ in call], [p for _, p in call], pieces, scal, *tables, vmem_bytes)
+            project([b for b, _ in call], [p for _, p in call], pieces, scal, *tables, vmem_bytes, space)
         )
 
     pair_place = planes[1] * rows
@@ -427,7 +430,7 @@
     made[1] = after(made[1], on3)
     partial = attend_blocks(made, parts, near_places, lengths[0] - side * rows, side, rows)
     far1, on3, far2, on4 = [after(x, *partial) for x in (far1, on3, far2, on4)]
-    run([((far1, on3), far_end * rows), ((far2, on4), far_end * rows + half)], VMEM_BYTES // 2)
+    run([((far1, on3), far_end * rows), ((far2, on4), far_end * rows + half)], SMALL_BYTES, pltpu.VMEM)
     return attend_blocks(made, parts, places, lengths[0], side, rows, partial)[0]
 
 

time: 301 us -> 300 us (level)
    unnamed x48 -> x46, local copies, waits for them, and re-layouts: 15.5 us -> 14.4 us
  transfers between devices with their start and end apart: 18 -> 18, of which waited for: 9 -> 10; matrix products, arithmetic and copies ran while one was open for 2% -> 2% of each run, Pallas kernels for 13% -> 13%
where the time goes in v1:
time: 300 us; the launch traced here: 294 us
  waiting for transfers between devices  147 us (49%)
  Pallas kernels  60.1 us (20%)
  starting transfers between devices  46.4 us (15%)
  local copies, waits for them, and re-layouts  22 us (7%)
  between operations  14.5 us (5%)
  other arithmetic  3.63 us (1%)
    ppermute x14, waiting for transfers between devices, across(): return lax.ppermute(x, 'tensor', pairs)  144 us
    ppermute x14, starting transfers between devices, across(): return lax.ppermute(x, 'tensor', pairs)  46.3 us
    pallas_call x3, Pallas kernels, project(): pl.pallas_call(functools.partial(project_kernel, counts, sources, tile),...  37.6 us
    pallas_call x2, Pallas kernels, attend_blocks(): pl.pallas_call(functools.partial(body, parts, block), out_shape=out_shape...  22.5 us
    unnamed x46, local copies, waits for them, and re-layouts  14.4 us
  transfers between devices with their start and end apart: 18, of which 10 were waited for; matrix products, arithmetic and copies ran while one was open for 2% of the time, Pallas kernels for 13%

profile of v1, /device:TPU:24, one launch (start us, length us, event | category | flops | bytes accessed | tf_op | source)
XLA Modules:
  0.0 294.2 jit_solution(15437501243413123987)
XLA Ops:
  6.5 4.2 %constant_dynamic-slice_fusion = (bf16[320,1536]{1,0:T(8,128)(2,1)}, bf16[320,1536]{1,0:T(8,128)(2,1)}, bf16[320,1536]{1,0:T(8,128)(2,1)}, bf16[320,1536]{1,0:T(8,128)(2,1)}) fusion(bf16[320,6144]{1,0:T(8,128)(2,1)} %param.7, s32[]{:T(128)S(6)} %select_n.26, s32[]{:T(128)S(6)} %select_n.24, s32[]{:T(128)S(6)} %select_n.23, s32[]{:T(128)S(6)} %select_n.25), kind=kLoop, calls=%fused_computation.13 | loop fusion | bytes 7864336 | tf_op jit(solution)/shard_map/dynamic_slice | solution.py:354
  10.8 0.0 all-gather.5.cloned.1.call-update
  10.8 0.0 all-gather.7.cloned.1.call-start
  10.9 0.6 fusion
  11.5 0.0 copy-done.20
  11.5 0.8 fusion.2.refs_0_.refs_4_
  12.3 0.9 fusion.4
  13.2 0.4 collective-permute-start.3
  13.7 0.5 copy-done.19
  14.2 0.3 collective-permute-start.1
  14.6 1.0 collective-permute-start
  15.6 3.0 %collective-permute-start.2 = (bf16[320,1536]{1,0:T(8,128)(2,1)}, bf16[320,1536]{1,0:T(8,128)(2,1)}, u32[]{:S(2)}, u32[]{:S(2)}) collective-permute-start(bf16[320,1536]{1,0:T(8,128)(2,1)} %get-tuple-element.52), channel_id=1, source_target_pairs={{0,3},{1,2},{2,1},{3,0},{4,7},{5,6},{6,5},{7,4},{8,11},{9,10},{10,... | collective-permute-start | bytes 2949128 | tf_op jit(solution)/shard_map/ppermute | solution.py:357
  18.6 2.0 fusion.5
  20.6 1.9 fusion.3
  22.6 0.3 pad_maximum_fusion
  22.9 19.9 %collective-permute-done.3.refs_1_.refs_5_ = bf16[64,5120]{1,0:T(8,128)(2,1)S(1)} collective-permute-done((bf16[64,5120]{1,0:T(8,128)(2,1)S(1)}, bf16[64,5120]{1,0:T(8,128)(2,1)S(1)}, u32[]{:S(2)}, u32[]{:S(2)}) %collective-permute-start.3) | collective-permute-done | bytes 655392 | tf_op jit(solution)/shard_map/ppermute | solution.py:357
  42.8 18.1 %collective-permute-done.1 = bf16[320,1536]{1,0:T(8,128)(2,1)} collective-permute-done((bf16[320,1536]{1,0:T(8,128)(2,1)S(1)}, bf16[320,1536]{1,0:T(8,128)(2,1)}, u32[]{:S(2)}, u32[]{:S(2)}) %collective-permute-start.1) | collective-permute-done | bytes 983072 | tf_op jit(solution)/shard_map/ppermute | solution.py:357
  61.0 32.0 %collective-permute-done = bf16[320,1536]{1,0:T(8,128)(2,1)} collective-permute-done((bf16[320,1536]{1,0:T(8,128)(2,1)}, bf16[320,1536]{1,0:T(8,128)(2,1)}, u32[]{:S(2)}, u32[]{:S(2)}) %collective-permute-start) | collective-permute-done | bytes 983072 | tf_op jit(solution)/shard_map/ppermute | solution.py:357
  93.0 0.0 all-gather.7.cloned.1.call-update
  93.0 0.0 all-gather.9.cloned.1.call-start
  93.1 0.7 all-gather.9.cloned.1.call-update
  93.8 0.0 all-gather.11.cloned.1.call-start
  93.8 0.5 all-gather.11.cloned.1.call-update
  94.4 9.6 %collective-permute-start.4 = (bf16[128,5120]{1,0:T(8,128)(2,1)}, bf16[128,5120]{1,0:T(8,128)(2,1)S(1)}, u32[]{:S(2)}, u32[]{:S(2)}) collective-permute-start(bf16[128,5120]{1,0:T(8,128)(2,1)} %get-tuple-element.28), channel_id=1, source_target_pairs={{0,1},{1,0},{2,3},{3,2},{4,5},{5,4},{6,7},{7,6},{8,9},{9,8},{10,11... | collective-permute-start | bytes 3932168 | tf_op jit(solution)/shard_map/ppermute | solution.py:357
  104.0 0.7 collective-permute-start.6
  104.7 27.4 %collective-permute-done.4.refs_2_.refs_6_ = bf16[128,5120]{1,0:T(8,128)(2,1)S(1)} collective-permute-done((bf16[128,5120]{1,0:T(8,128)(2,1)}, bf16[128,5120]{1,0:T(8,128)(2,1)S(1)}, u32[]{:S(2)}, u32[]{:S(2)}) %collective-permute-start.4) | collective-permute-done | bytes 1310752 | tf_op jit(solution)/shard_map/ppermute | solution.py:357
  132.1 1.1 copy-done.12
  133.2 0.7 collective-permute-start.7
  133.9 3.9 %collective-permute-start.5 = (bf16[64,5120]{1,0:T(8,128)(2,1)}, bf16[64,5120]{1,0:T(8,128)(2,1)S(1)}, u32[]{:S(2)}, u32[]{:S(2)}) collective-permute-start(bf16[64,5120]{1,0:T(8,128)(2,1)} %get-tuple-element.30), channel_id=1, source_target_pairs={{0,1},{1,0},{2,3},{3,2},{4,5},{5,4},{6,7},{7,6},{8,9},{9,8},{10,11... | collective-permute-start | bytes 1966088 | tf_op jit(solution)/shard_map/ppermute | solution.py:357
  137.9 1.3 collective-permute-start.8
  139.1 1.1 copy-done.6
  140.2 13.5 %collective-permute-done.5.refs_3_.refs_7_ = bf16[64,5120]{1,0:T(8,128)(2,1)S(1)} collective-permute-done((bf16[64,5120]{1,0:T(8,128)(2,1)}, bf16[64,5120]{1,0:T(8,128)(2,1)S(1)}, u32[]{:S(2)}, u32[]{:S(2)}) %collective-permute-start.5) | collective-permute-done | bytes 655392 | tf_op jit(solution)/shard_map/ppermute | solution.py:357
  153.7 0.9 copy-done.14
  154.6 15.0 %collective-permute-start.10 = (bf16[128,5120]{1,0:T(8,128)(2,1)}, bf16[128,5120]{1,0:T(8,128)(2,1)}, u32[]{:S(2)}, u32[]{:S(2)}) collective-permute-start(bf16[128,5120]{1,0:T(8,128)(2,1)} %get-tuple-element.39), channel_id=1, source_target_pairs={{0,2},{3,1},{4,6},{7,5},{8,10},{11,9},{12,14},{15,13},{16,18},{19,... | collective-permute-start | bytes 3932168 | tf_op jit(solution)/shard_map/ppermute | solution.py:357
  169.5 1.3 collective-permute-start.9
  170.8 11.0 %collective-permute-done.8.refs_2_ = bf16[128,5120]{1,0:T(8,128)(2,1)S(1)} collective-permute-done((bf16[128,5120]{1,0:T(8,128)(2,1)S(1)}, bf16[128,5120]{1,0:T(8,128)(2,1)S(1)}, u32[]{:S(2)}, u32[]{:S(2)}) %collective-permute-start.8) | collective-permute-done | bytes 1310752 | tf_op jit(solution)/shard_map/ppermute | solution.py:357
  181.8 1.1 copy-done.10
  182.9 11.8 %collective-permute-done.10.refs_0_ = bf16[128,5120]{1,0:T(8,128)(2,1)} collective-permute-done((bf16[128,5120]{1,0:T(8,128)(2,1)}, bf16[128,5120]{1,0:T(8,128)(2,1)}, u32[]{:S(2)}, u32[]{:S(2)}) %collective-permute-start.10) | collective-permute-done | bytes 1310752 | tf_op jit(solution)/shard_map/ppermute | solution.py:357
  194.6 6.3 %collective-permute-start.12 = (bf16[128,5120]{1,0:T(8,128)(2,1)}, bf16[128,5120]{1,0:T(8,128)(2,1)}, u32[]{:S(2)}, u32[]{:S(2)}) collective-permute-start(bf16[128,5120]{1,0:T(8,128)(2,1)} %get-tuple-element.44), channel_id=1, source_target_pairs={{0,2},{3,1},{4,6},{7,5},{8,10},{11,9},{12,14},{15,13},{16,18},{19,... | collective-permute-start | bytes 3932168 | tf_op jit(solution)/shard_map/ppermute | solution.py:357
  201.0 0.1 concatenate.18.scal
  201.1 1.3 collective-permute-start.11
  202.4 0.0 all-gather.5.cloned.1.call-done.refs_8_.refs_4_
  202.4 0.0 all-gather.7.cloned.1.call-done.refs_9_.refs_5_
  202.4 0.0 all-gather.9.cloned.1.call-done.refs_10_.refs_6_
  202.5 1.9 all-gather.11.cloned.1.call-done.refs_11_.refs_7_
  204.3 1.3 copy-done.13
  205.6 1.1 copy-done.15
  206.7 16.4 %project.3.refs_0_ = bf16[512,1536]{1,0:T(8,128)(2,1)} custom-call(s32[13]{0:T(128)S(1)} %concatenate.18.scal, bf16[256,5120]{1,0:T(8,128)(2,1)} %copy-done.16, bf16[64,5120]{1,0:T(8,128)(2,1)S(1)} %collective-permute-done.3.refs_1_.refs_5_, bf16[128,5120]{1,0:T(8,128)(2,1)S(1)} %copy-done.13, bf16[64,5120]{1,0:T(8,128)(2,1)S(1)} %copy-done.15, ...), custom_call_target="tpu_custom_call" | custom-call | flops 8053063680 | bytes 22544384 | tf_op jit(solution)/shard_map/project/pallas_call | solution.py:158
  223.2 1.9 collective-permute-done.12.refs_1_
  225.1 1.3 collective-permute-start.13
  227.1 0.1 concatenate.22.scal
  227.2 0.1 concatenate.21.scal
  227.3 0.1 stack.97.scal
  227.3 0.1 stack.113.scal
  227.4 1.3 copy-done.7
  228.8 1.3 copy-done.9
  230.1 1.3 copy-done.11
  231.4 12.1 %project.4.refs_1_ = bf16[256,1536]{1,0:T(8,128)(2,1)} custom-call(s32[11]{0:T(128)S(1)} %concatenate.21.scal, bf16[128,5120]{1,0:T(8,128)(2,1)S(1)} %copy-done.7, bf16[128,5120]{1,0:T(8,128)(2,1)S(1)} %copy-done.9, bf16[128,5120]{1,0:T(8,128)(2,1)S(1)} %copy-done.11, bf16[128,5120]{1,0:T(8,128)(2,1)} %collective-permute-done.9.refs_3_, ...), custom_call_target="tpu_custom_call" | custom-call | flops 4026531840 | bytes 19136512 | tf_op jit(solution)/shard_map/project/pallas_call | solution.py:158
  243.6 1.3 copy-done.4
  244.9 10.1 %attend_near.1 = (f32[768,1024]{1,0:T(8,128)S(1)}, f32[768,128]{1,0:T(8,128)S(1)}) custom-call(s32[8]{0:T(128)S(1)} %stack.113.scal, bf16[512,1536]{1,0:T(8,128)(2,1)S(1)} %copy-done.5, bf16[256,1536]{1,0:T(8,128)(2,1)S(1)} %copy-done.4), custom_call_target="tpu_custom_call" | custom-call | flops 1207959552 | bytes 3932160 | tf_op jit(solution)/shard_map/attend_near/pallas_call | solution.py:319
  255.0 8.6 %collective-permute-done.13.refs_3_ = bf16[128,5120]{1,0:T(8,128)(2,1)} collective-permute-done((bf16[128,5120]{1,0:T(8,128)(2,1)}, bf16[128,5120]{1,0:T(8,128)(2,1)}, u32[]{:S(2)}, u32[]{:S(2)}) %collective-permute-start.13) | collective-permute-done | bytes 1310752 | tf_op jit(solution)/shard_map/ppermute | solution.py:357
  263.6 2.1 copy-done.3
  265.7 9.0 %project.5.refs_2_ = bf16[256,1536]{1,0:T(8,128)(2,1)S(1)} custom-call(s32[11]{0:T(128)S(1)} %concatenate.22.scal, bf16[128,5120]{1,0:T(8,128)(2,1)} %collective-permute-done.10.refs_0_, bf16[128,5120]{1,0:T(8,128)(2,1)} %collective-permute-done.12.refs_1_, bf16[128,5120]{1,0:T(8,128)(2,1)} %collective-permute-done.11.refs_2_, ...), custom_call_target="tpu_custom_call" | custom-call | flops 4026531840 | bytes 19136512 | tf_op jit(solution)/shard_map/project/pallas_call | solution.py:158
  274.8 12.4 %attend_far.1 = bf16[1024,1024]{1,0:T(8,128)(2,1)} custom-call(s32[10]{0:T(128)S(1)} %stack.97.scal, bf16[512,1536]{1,0:T(8,128)(2,1)S(1)} %copy-done.5, bf16[256,1536]{1,0:T(8,128)(2,1)S(1)} %copy-done.4, bf16[256,1536]{1,0:T(8,128)(2,1)S(1)} %project.5.refs_2_, f32[768,1024]{1,0:T(8,128)S(1)} %get-tuple-element.41.refs_3_, ...), custom_call_target="tpu_custom_call" | custom-call | flops 2147483648 | bytes 5242880 | tf_op jit(solution)/shard_map/attend_far/pallas_call | solution.py:319
  (43 shorter events, 0.1 us)
Async XLA Ops:
  6.5 195.9 %all-gather.5.cloned.1.call-start = ((), (), s32[]{:S(2)}) async-start(), calls=%async_computation | async-start | bytes 4915200 | tf_op jit(solution)/shard_map/all_gather | solution.py:363
  6.5 4.3 %copy-start.17 = (bf16[256,5120]{1,0:T(8,128)(2,1)S(1)}, bf16[256,5120]{1,0:T(8,128)(2,1)}, u32[]{:S(2)}) copy-start(bf16[256,5120]{1,0:T(8,128)(2,1)} %param.6) | copy-start | bytes 7864324
  10.8 0.7 copy-start.20
  10.8 191.6 %all-gather.7.cloned.1.call-start = ((), (), s32[]{:S(2)}) async-start(), calls=%async_computation.1 | async-start | bytes 4915200 | tf_op jit(solution)/shard_map/all_gather | solution.py:363
  12.3 8.3 %copy-start.16 = (bf16[256,5120]{1,0:T(8,128)(2,1)}, bf16[256,5120]{1,0:T(8,128)(2,1)S(1)}, u32[]{:S(2)}) copy-start(bf16[256,5120]{1,0:T(8,128)(2,1)S(1)} %fusion.2.refs_0_.refs_4_) | copy-start | bytes 7864324
  12.3 1.9 copy-start.19
  13.2 29.6 %collective-permute-start.3 = (bf16[64,5120]{1,0:T(8,128)(2,1)S(1)}, bf16[64,5120]{1,0:T(8,128)(2,1)S(1)}, u32[]{:S(2)}, u32[]{:S(2)}) collective-permute-start(bf16[64,5120]{1,0:T(8,128)(2,1)S(1)} %get-tuple-element.54), channel_id=1, source_target_pairs={{0,1},{1,0},{2,3},{3,2},{4,5},{5,4},{6,7},{7,6},{8,9},{9,8},{10,11... | collective-permute-start | bytes 1966088 | tf_op jit(solution)/shard_map/ppermute | solution.py:357
  14.2 46.8 %collective-permute-start.1 = (bf16[320,1536]{1,0:T(8,128)(2,1)S(1)}, bf16[320,1536]{1,0:T(8,128)(2,1)}, u32[]{:S(2)}, u32[]{:S(2)}) collective-permute-start(bf16[320,1536]{1,0:T(8,128)(2,1)S(1)} %copy-done.19), channel_id=1, source_target_pairs={{0,2},{1,3},{2,0},{3,1},{4,6},{5,7},{6,4},{7,5},{8,10},{9,11},{10,... | collective-permute-start | bytes 2949128 | tf_op jit(solution)/shard_map/ppermute | solution.py:357
  14.6 78.4 %collective-permute-start = (bf16[320,1536]{1,0:T(8,128)(2,1)}, bf16[320,1536]{1,0:T(8,128)(2,1)}, u32[]{:S(2)}, u32[]{:S(2)}) collective-permute-start(bf16[320,1536]{1,0:T(8,128)(2,1)} %get-tuple-element.51), channel_id=1, source_target_pairs={{0,1},{1,0},{2,3},{3,2},{4,5},{5,4},{6,7},{7,6},{8,9},{9,8},{10,11... | collective-permute-start | bytes 2949128 | tf_op jit(solution)/shard_map/ppermute | solution.py:357
  15.6 77.4 %collective-permute-start.2 = (bf16[320,1536]{1,0:T(8,128)(2,1)}, bf16[320,1536]{1,0:T(8,128)(2,1)}, u32[]{:S(2)}, u32[]{:S(2)}) collective-permute-start(bf16[320,1536]{1,0:T(8,128)(2,1)} %get-tuple-element.52), channel_id=1, source_target_pairs={{0,3},{1,2},{2,1},{3,0},{4,7},{5,6},{6,5},{7,4},{8,11},{9,10},{10,... | collective-permute-start | bytes 2949128 | tf_op jit(solution)/shard_map/ppermute | solution.py:357
  22.6 178.5 %copy-start.21 = (f32[128]{0:T(128)S(1)}, f32[128]{0:T(128)}, u32[]{:S(2)}) copy-start(f32[128]{0:T(128)} %param.10) | copy-start | bytes 1540
  22.6 178.5 %copy-start.22 = (f32[128]{0:T(128)S(1)}, f32[128]{0:T(128)}, u32[]{:S(2)}) copy-start(f32[128]{0:T(128)} %param.9) | copy-start | bytes 1540
  22.9 81.1 %copy-start.18 = (bf16[128,5120]{1,0:T(8,128)(2,1)S(1)}, bf16[128,5120]{1,0:T(8,128)(2,1)}, u32[]{:S(2)}) copy-start(bf16[128,5120]{1,0:T(8,128)(2,1)} %get-tuple-element.39) | copy-start | bytes 3932164
  93.0 109.4 %all-gather.9.cloned.1.call-start = ((), (), s32[]{:S(2)}) async-start(), calls=%async_computation.2 | async-start | bytes 4915200 | tf_op jit(solution)/shard_map/all_gather | solution.py:363
  93.8 110.5 %all-gather.11.cloned.1.call-start = ((), (), s32[]{:S(2)}) async-start(), calls=%async_computation.3 | async-start | bytes 4915200 | tf_op jit(solution)/shard_map/all_gather | solution.py:363
  94.4 37.8 %collective-permute-start.4 = (bf16[128,5120]{1,0:T(8,128)(2,1)}, bf16[128,5120]{1,0:T(8,128)(2,1)S(1)}, u32[]{:S(2)}, u32[]{:S(2)}) collective-permute-start(bf16[128,5120]{1,0:T(8,128)(2,1)} %get-tuple-element.28), channel_id=1, source_target_pairs={{0,1},{1,0},{2,3},{3,2},{4,5},{5,4},{6,7},{7,6},{8,9},{9,8},{10,11... | collective-permute-start | bytes 3932168 | tf_op jit(solution)/shard_map/ppermute | solution.py:357
  104.0 29.2 %collective-permute-start.6 = (bf16[128,5120]{1,0:T(8,128)(2,1)S(1)}, bf16[128,5120]{1,0:T(8,128)(2,1)S(1)}, u32[]{:S(2)}, u32[]{:S(2)}) collective-permute-start(bf16[128,5120]{1,0:T(8,128)(2,1)S(1)} %copy-done.18), channel_id=1, source_target_pairs={{1,2},{2,1},{5,6},{6,5},{9,10},{10,9},{13,14},{14,13},{17,18},{18,... | collective-permute-start | bytes 3932168 | tf_op jit(solution)/shard_map/ppermute | solution.py:357
  132.1 1.1 copy-start.12
  133.2 21.4 %collective-permute-start.7 = (bf16[128,5120]{1,0:T(8,128)(2,1)}, bf16[128,5120]{1,0:T(8,128)(2,1)S(1)}, u32[]{:S(2)}, u32[]{:S(2)}) collective-permute-start(bf16[128,5120]{1,0:T(8,128)(2,1)} %get-tuple-element.44), channel_id=1, source_target_pairs={{1,2},{2,1},{5,6},{6,5},{9,10},{10,9},{13,14},{14,13},{17,18},{18,... | collective-permute-start | bytes 3932168 | tf_op jit(solution)/shard_map/ppermute | solution.py:357
  133.9 19.8 %collective-permute-start.5 = (bf16[64,5120]{1,0:T(8,128)(2,1)}, bf16[64,5120]{1,0:T(8,128)(2,1)S(1)}, u32[]{:S(2)}, u32[]{:S(2)}) collective-permute-start(bf16[64,5120]{1,0:T(8,128)(2,1)} %get-tuple-element.30), channel_id=1, source_target_pairs={{0,1},{1,0},{2,3},{3,2},{4,5},{5,4},{6,7},{7,6},{8,9},{9,8},{10,11... | collective-permute-start | bytes 1966088 | tf_op jit(solution)/shard_map/ppermute | solution.py:357
  137.9 43.9 %collective-permute-start.8 = (bf16[128,5120]{1,0:T(8,128)(2,1)S(1)}, bf16[128,5120]{1,0:T(8,128)(2,1)S(1)}, u32[]{:S(2)}, u32[]{:S(2)}) collective-permute-start(bf16[128,5120]{1,0:T(8,128)(2,1)S(1)} %collective-permute-done.6.refs_0_), channel_id=1, source_target_pairs={{1,0},{2,3},{5,4},{6,7},{9,8},{10,11},{13,12},{14,15},{17,16},{18,... | collective-permute-start | bytes 3932168 | tf_op jit(solution)/shard_map/ppermute | solution.py:357
  139.1 1.1 copy-start.6
  153.7 0.9 copy-start.14
  154.6 68.6 %copy-start.8 = (bf16[128,5120]{1,0:T(8,128)(2,1)}, bf16[128,5120]{1,0:T(8,128)(2,1)S(1)}, u32[]{:S(2)}) copy-start(bf16[128,5120]{1,0:T(8,128)(2,1)S(1)} %collective-permute-done.7.refs_1_) | copy-start | bytes 3932164
  154.6 40.0 %collective-permute-start.10 = (bf16[128,5120]{1,0:T(8,128)(2,1)}, bf16[128,5120]{1,0:T(8,128)(2,1)}, u32[]{:S(2)}, u32[]{:S(2)}) collective-permute-start(bf16[128,5120]{1,0:T(8,128)(2,1)} %get-tuple-element.39), channel_id=1, source_target_pairs={{0,2},{3,1},{4,6},{7,5},{8,10},{11,9},{12,14},{15,13},{16,18},{19,... | collective-permute-start | bytes 3932168 | tf_op jit(solution)/shard_map/ppermute | solution.py:357
  169.5 53.6 %collective-permute-start.9 = (bf16[128,5120]{1,0:T(8,128)(2,1)S(1)}, bf16[128,5120]{1,0:T(8,128)(2,1)}, u32[]{:S(2)}, u32[]{:S(2)}) collective-permute-start(bf16[128,5120]{1,0:T(8,128)(2,1)S(1)} %collective-permute-done.7.refs_1_), channel_id=1, source_target_pairs={{1,0},{2,3},{5,4},{6,7},{9,8},{10,11},{13,12},{14,15},{17,16},{18,... | collective-permute-start | bytes 3932168 | tf_op jit(solution)/shard_map/ppermute | solution.py:357
  181.8 1.1 copy-start.10
  194.6 30.5 %collective-permute-start.12 = (bf16[128,5120]{1,0:T(8,128)(2,1)}, bf16[128,5120]{1,0:T(8,128)(2,1)}, u32[]{:S(2)}, u32[]{:S(2)}) collective-permute-start(bf16[128,5120]{1,0:T(8,128)(2,1)} %get-tuple-element.44), channel_id=1, source_target_pairs={{0,2},{3,1},{4,6},{7,5},{8,10},{11,9},{12,14},{15,13},{16,18},{19,... | collective-permute-start | bytes 3932168 | tf_op jit(solution)/shard_map/ppermute | solution.py:357
  201.1 42.5 %collective-permute-start.11 = (bf16[128,5120]{1,0:T(8,128)(2,1)}, bf16[128,5120]{1,0:T(8,128)(2,1)}, u32[]{:S(2)}, u32[]{:S(2)}) collective-permute-start(bf16[128,5120]{1,0:T(8,128)(2,1)} %collective-permute-done.10.refs_0_), channel_id=1, source_target_pairs={{1,0},{2,3},{5,4},{6,7},{9,8},{10,11},{13,12},{14,15},{17,16},{18,... | collective-permute-start | bytes 3932168 | tf_op jit(solution)/shard_map/ppermute | solution.py:357
  204.3 1.3 copy-start.13
  205.6 1.1 copy-start.15
  225.1 38.5 %collective-permute-start.13 = (bf16[128,5120]{1,0:T(8,128)(2,1)}, bf16[128,5120]{1,0:T(8,128)(2,1)}, u32[]{:S(2)}, u32[]{:S(2)}) collective-permute-start(bf16[128,5120]{1,0:T(8,128)(2,1)} %collective-permute-done.12.refs_1_), channel_id=1, source_target_pairs={{1,0},{2,3},{5,4},{6,7},{9,8},{10,11},{13,12},{14,15},{17,16},{18,... | collective-permute-start | bytes 3932168 | tf_op jit(solution)/shard_map/ppermute | solution.py:357
  227.4 1.3 copy-start.7
  228.8 1.3 copy-start.9
  230.1 1.3 copy-start.11
  231.4 12.2 %copy-start.5 = (bf16[512,1536]{1,0:T(8,128)(2,1)S(1)}, bf16[512,1536]{1,0:T(8,128)(2,1)}, u32[]{:S(2)}) copy-start(bf16[512,1536]{1,0:T(8,128)(2,1)} %project.3.refs_0_) | copy-start | bytes 4718596
  231.4 32.2 %copy-start.1 = (bf16[1280,1536]{1,0:T(8,128)(2,1)S(1)}, bf16[1280,1536]{1,0:T(8,128)(2,1)}, u32[]{:S(2)}) copy-start(bf16[1280,1536]{1,0:T(8,128)(2,1)} %all-gather.7.cloned.1.call-done.refs_9_.refs_5_) | copy-start | bytes 11796484
  231.4 32.2 %copy-start.2 = (bf16[1280,1536]{1,0:T(8,128)(2,1)S(1)}, bf16[1280,1536]{1,0:T(8,128)(2,1)}, u32[]{:S(2)}) copy-start(bf16[1280,1536]{1,0:T(8,128)(2,1)} %all-gather.9.cloned.1.call-done.refs_10_.refs_6_) | copy-start | bytes 11796484
  243.5 20.1 %copy-start = (bf16[1280,1536]{1,0:T(8,128)(2,1)S(1)}, bf16[1280,1536]{1,0:T(8,128)(2,1)}, u32[]{:S(2)}) copy-start(bf16[1280,1536]{1,0:T(8,128)(2,1)} %all-gather.5.cloned.1.call-done.refs_8_.refs_4_) | copy-start | bytes 11796484
  243.6 1.3 copy-start.4
  263.6 2.1 copy-start.3
Sparse Core Ops, SparseCore 0:
  10.9 33.9 all-gather.4
  93.2 42.0 all-gather.6
  136.8 32.9 all-gather.8
  171.3 32.9 all-gather.10

commit v2 on v1

--- a/solution.py
+++ b/solution.py
@@ -212,63 +212,62 @@
     )
 
 
-def attend_rows(held, head, low, block, length):
+def attend_rows(own, at, rest, head, position, length):
     query_at, key_at, value_at, _ = head_columns(head)
-    high = low + block
+    block = at.stop - at.start
     row = lax.broadcasted_iota(jnp.int32, (block, block), 0)
     col = lax.broadcasted_iota(jnp.int32, (block, block), 1)
-    query = held[low:high, query_at]
-    last = lax.dot_general(
-        query, held[low:high, key_at], CONTRACT, preferred_element_type=jnp.float32
-    )
-    last = jnp.where((col <= row) & (col + low < length), last, -1e30)
+    query = own[at, query_at]
+    last = lax.dot_general(query, own[at, key_at], CONTRACT, preferred_element_type=jnp.float32)
+    last = jnp.where((col <= row) & (col + position < length), last, -1e30)
     top = jnp.max(last, axis=-1, keepdims=True)
-    if low:
-        rest = lax.dot_general(
-            query, held[:low, key_at], CONTRACT, preferred_element_type=jnp.float32
+    if position:
+        before = lax.dot_general(
+            query, rest[:position, key_at], CONTRACT, preferred_element_type=jnp.float32
         )
-        keys = lax.broadcasted_iota(jnp.int32, (1, low), 1)
-        rest = rest + jnp.where(keys < length, 0.0, -1e30)
-        top = jnp.maximum(top, jnp.max(rest, axis=-1, keepdims=True))
+        keys = lax.broadcasted_iota(jnp.int32, (1, position), 1)
+        before = before + jnp.where(keys < length, 0.0, -1e30)
+        top = jnp.maximum(top, jnp.max(before, axis=-1, keepdims=True))
     probs = jnp.exp2((last - top) * FACTOR)
     norm = jnp.sum(probs, axis=-1, keepdims=True)
     value = jnp.dot(
-        probs.astype(jnp.bfloat16), held[low:high, value_at], preferred_element_type=jnp.float32
-    )
-    if low:
-        probs = jnp.exp2((rest - top) * FACTOR)
+        probs.astype(jnp.bfloat16), own[at, value_at], preferred_element_type=jnp.float32
+    )
+    if position:
+        probs = jnp.exp2((before - top) * FACTOR)
         norm = norm + jnp.sum(probs, axis=-1, keepdims=True)
         value = value + jnp.dot(
-            probs.astype(jnp.bfloat16), held[:low, value_at], preferred_element_type=jnp.float32
+            probs.astype(jnp.bfloat16),
+            rest[:position, value_at],
+            preferred_element_type=jnp.float32,
         )
     return top, norm, value
 
 
 def attend_near_kernel(parts, block, scal, *refs):
     partial, stats, held, sems = refs[len(parts) :]
-    fetch_blocks(refs, parts, lambda number: scal[2 + number], held, sems)
-    heads = partial.shape[1] // HD
-    for head in range(heads):
+    fetch_blocks(refs, parts, lambda number: scal[1 + number], held, sems)
+    for head in range(partial.shape[1] // HD):
         out_at = head_columns(head)[3]
         for low in range(0, held.shape[0], block):
-            top, norm, value = attend_rows(held, head, low, block, scal[0])
-            partial[low : low + block, out_at] = value / norm
-            stats[low : low + block, head : head + 1] = top * FACTOR + jnp.log(norm) * LOG2E
-
-
-def attend_far_kernel(parts, block, scal, *refs):
-    partial, stats, out, held, sems = refs[len(parts) :]
-    fetch_blocks(refs, parts, lambda number: scal[2 + number], held, sems)
+            at = slice(low, low + block)
+            top, norm, value = attend_rows(held, at, held, head, low, scal[0])
+            partial[at, out_at] = value / norm
+            stats[at, head : head + 1] = top * FACTOR + jnp.log(norm) * LOG2E
+
+
+def attend_far_kernel(scal, far, held, partial, stats, out):
     heads = out.shape[1] // HD
-    total = held.shape[0]
+    block = far.shape[0]
+    low = held.shape[0]
+    whole = slice(0, block)
     length = scal[0]
 
     @pl.when(scal[1] == 0)
     def _():
-        low = total - block
         for head in range(heads):
             out_at = head_columns(head)[3]
-            _, norm, value = attend_rows(held, head, low, block, length)
+            _, norm, value = attend_rows(far, whole, held, head, low, length)
             out[low:, out_at] = (value / norm).astype(out.dtype)
         out[:low, :] = partial[...].astype(out.dtype)
 
@@ -276,13 +275,10 @@
     def _():
         for head in range(heads):
             query_at, key_at, value_at, out_at = head_columns(head)
-            _, norm, value = attend_rows(held, head, 0, block, length)
+            _, norm, value = attend_rows(far, whole, far, head, 0, length)
             out[:block, out_at] = (value / norm).astype(out.dtype)
             scores = lax.dot_general(
-                held[block:, query_at],
-                held[:block, key_at],
-                CONTRACT,
-                preferred_element_type=jnp.float32,
+                held[:, query_at], far[:, key_at], CONTRACT, preferred_element_type=jnp.float32
             )
             keys = lax.broadcasted_iota(jnp.int32, (1, block), 1)
             scores = scores * FACTOR + jnp.where(keys < length, 0.0, -1e30)
@@ -292,49 +288,56 @@
             scale = jnp.exp2(before - top)
             norm = scale + jnp.sum(probs, axis=-1, keepdims=True)
             value = partial[:, out_at] * scale + jnp.dot(
-                probs.astype(jnp.bfloat16),
-                held[:block, value_at],
-                preferred_element_type=jnp.float32,
+                probs.astype(jnp.bfloat16), far[:, value_at], preferred_element_type=jnp.float32
             )
             out[block:, out_at] = (value / norm).astype(out.dtype)
 
 
-def attend_blocks(arrays, parts, places, length, side, block, partial=None):
+def attend_cost(rows, wide):
+    return pl.CostEstimate(
+        flops=2 * rows * rows * wide,
+        bytes_accessed=4 * rows * wide,
+        transcendentals=rows * rows * wide // HD // 2,
+    )
+
+
+def attend_near(arrays, parts, places, length, block):
     rows = sum(a.shape[0] for a in arrays)
     columns = arrays[0].shape[1]
     wide = columns // (GQ + 2) * GQ
-    scal = jnp.stack([length, side] + list(places)).astype(jnp.int32)
-    hbm = pl.BlockSpec(memory_space=pltpu.HBM)
+    scal = jnp.stack([length] + list(places)).astype(jnp.int32)
     vmem = pl.BlockSpec(memory_space=pltpu.VMEM)
-    if partial is None:
-        body, name = attend_near_kernel, "attend_near"
-        out_shape = [
+    return pl.pallas_call(
+        functools.partial(attend_near_kernel, parts, block),
+        out_shape=[
             jax.ShapeDtypeStruct((rows, wide), jnp.float32),
             jax.ShapeDtypeStruct((rows, HD), jnp.float32),
-        ]
-    else:
-        body, name = attend_far_kernel, "attend_far"
-        out_shape = [jax.ShapeDtypeStruct((rows, wide), jnp.bfloat16)]
-    extra = [] if partial is None else list(partial)
+            jax.ShapeDtypeStruct((rows, columns), jnp.bfloat16),
+        ],
+        in_specs=[pl.BlockSpec(memory_space=pltpu.SMEM)]
+        + [pl.BlockSpec(memory_space=pltpu.HBM)] * len(arrays),
+        out_specs=[vmem] * 3,
+        scratch_shapes=[pltpu.SemaphoreType.DMA((len(places),))],
+        compiler_params=pltpu.CompilerParams(vmem_limit_bytes=SMALL_BYTES),
+        cost_estimate=attend_cost(rows, wide),
+        name="attend_near",
+    )(scal, *arrays)
+
+
+def attend_far(far, near, length, side):
+    partial, stats, held = near
+    rows = far.shape[0] + held.shape[0]
+    wide = partial.shape[1]
+    vmem = pl.BlockSpec(memory_space=pltpu.VMEM)
     return pl.pallas_call(
-        functools.partial(body, parts, block),
-        out_shape=out_shape,
-        in_specs=[pl.BlockSpec(memory_space=pltpu.SMEM)]
-        + [hbm] * len(arrays)
-        + [vmem] * len(extra),
-        out_specs=[vmem] * len(out_shape),
-        scratch_shapes=[
-            pltpu.VMEM((rows, columns), jnp.bfloat16),
-            pltpu.SemaphoreType.DMA((len(places),)),
-        ],
+        attend_far_kernel,
+        out_shape=jax.ShapeDtypeStruct((rows, wide), jnp.bfloat16),
+        in_specs=[pl.BlockSpec(memory_space=pltpu.SMEM)] + [vmem] * 4,
+        out_specs=vmem,
         compiler_params=pltpu.CompilerParams(vmem_limit_bytes=SMALL_BYTES),
-        cost_estimate=pl.CostEstimate(
-            flops=2 * rows * rows * wide,
-            bytes_accessed=2 * rows * (columns + wide),
-            transcendentals=rows * rows * wide // HD // 2,
-        ),
-        name=name,
-    )(scal, *arrays, *extra)
+        cost_estimate=attend_cost(rows, wide),
+        name="attend_far",
+    )(jnp.stack([length, side]).astype(jnp.int32), far, held, partial, stats)
 
 
 def after(x, *earlier):
@@ -428,10 +431,10 @@
     run([((swap1, on1), far_mid * rows), ((swap2, on2), far_mid * rows + half)])
     near_places = [place - side * rows for place in places]
     made[1] = after(made[1], on3)
-    partial = attend_blocks(made, parts, near_places, lengths[0] - side * rows, side, rows)
+    partial = attend_near(made, parts, near_places, lengths[0] - side * rows, rows)
     far1, on3, far2, on4 = [after(x, *partial) for x in (far1, on3, far2, on4)]
     run([((far1, on3), far_end * rows), ((far2, on4), far_end * rows + half)], SMALL_BYTES, pltpu.VMEM)
-    return attend_blocks(made, parts, places, lengths[0], side, rows, partial)[0]
+    return attend_far(made[-1], partial, lengths[0], side)
 
 
 def solution(mesh):

time: 300 us -> 298 us (level)
    unnamed x46 -> x36, local copies, waits for them, and re-layouts: 14.4 us -> 12.3 us
where the time goes in v2:
time: 298 us; the launch traced here: 293 us
  waiting for transfers between devices  149 us (50%)
  Pallas kernels  58.7 us (20%)
  starting transfers between devices  46.7 us (16%)
  local copies, waits for them, and re-layouts  19.8 us (7%)
  between operations  14.5 us (5%)
  other arithmetic  3.7 us (1%)
    ppermute x14, waiting for transfers between devices, across(): return lax.ppermute(x, 'tensor', pairs)  146 us
    ppermute x14, starting transfers between devices, across(): return lax.ppermute(x, 'tensor', pairs)  46.6 us
    pallas_call x3, Pallas kernels, project(): pl.pallas_call(functools.partial(project_kernel, counts, sources, tile),...  37.6 us
    unnamed x36, local copies, waits for them, and re-layouts  12.3 us
    pallas_call x1, Pallas kernels, attend_far(): pl.pallas_call(attend_far_kernel, out_shape=jax.ShapeDtypeStruct((rows, w...  10.9 us
    pallas_call x1, Pallas kernels, attend_near(): pl.pallas_call(functools.partial(attend_near_kernel, parts, block), out_s...  10.2 us
  transfers between devices with their start and end apart: 18, of which 10 were waited for; matrix products, arithmetic and copies ran while one was open for 2% of the time, Pallas kernels for 13%

profile of v2, /device:TPU:24, one launch (start us, length us, event | category | flops | bytes accessed | tf_op | source)
XLA Modules:
  0.0 292.8 jit_solution(2888641720476082394)
XLA Ops:
  6.5 4.2 %constant_dynamic-slice_fusion = (bf16[320,1536]{1,0:T(8,128)(2,1)}, bf16[320,1536]{1,0:T(8,128)(2,1)}, bf16[320,1536]{1,0:T(8,128)(2,1)}, bf16[320,1536]{1,0:T(8,128)(2,1)}) fusion(bf16[320,6144]{1,0:T(8,128)(2,1)} %param.7, s32[]{:T(128)S(6)} %select_n.26, s32[]{:T(128)S(6)} %select_n.24, s32[]{:T(128)S(6)} %select_n.23, s32[]{:T(128)S(6)} %select_n.25), kind=kLoop, calls=%fused_computation.13 | loop fusion | bytes 7864336 | tf_op jit(solution)/shard_map/dynamic_slice | solution.py:357
  10.8 0.0 all-gather.5.cloned.1.call-update
  10.8 0.0 all-gather.7.cloned.1.call-start
  10.9 0.6 fusion
  11.5 0.0 copy-done.15
  11.5 0.8 fusion.2.refs_0_.refs_4_
  12.3 0.0 copy-start.14
  12.3 0.9 fusion.4
  13.2 0.4 collective-permute-start.3
  13.7 0.5 copy-done.14
  14.2 0.3 collective-permute-start.1
  14.6 1.0 collective-permute-start
  15.6 3.0 %collective-permute-start.2 = (bf16[320,1536]{1,0:T(8,128)(2,1)}, bf16[320,1536]{1,0:T(8,128)(2,1)}, u32[]{:S(2)}, u32[]{:S(2)}) collective-permute-start(bf16[320,1536]{1,0:T(8,128)(2,1)} %get-tuple-element.54), channel_id=1, source_target_pairs={{0,3},{1,2},{2,1},{3,0},{4,7},{5,6},{6,5},{7,4},{8,11},{9,10},{10,... | collective-permute-start | bytes 2949128 | tf_op jit(solution)/shard_map/ppermute | solution.py:360
  18.6 2.0 fusion.5
  20.6 1.9 fusion.3
  22.6 0.0 copy-start.17
  22.6 0.3 pad_maximum_fusion
  22.9 19.9 %collective-permute-done.3.refs_1_.refs_5_ = bf16[64,5120]{1,0:T(8,128)(2,1)S(1)} collective-permute-done((bf16[64,5120]{1,0:T(8,128)(2,1)S(1)}, bf16[64,5120]{1,0:T(8,128)(2,1)S(1)}, u32[]{:S(2)}, u32[]{:S(2)}) %collective-permute-start.3) | collective-permute-done | bytes 655392 | tf_op jit(solution)/shard_map/ppermute | solution.py:360
  42.9 18.1 %collective-permute-done.1 = bf16[320,1536]{1,0:T(8,128)(2,1)} collective-permute-done((bf16[320,1536]{1,0:T(8,128)(2,1)S(1)}, bf16[320,1536]{1,0:T(8,128)(2,1)}, u32[]{:S(2)}, u32[]{:S(2)}) %collective-permute-start.1) | collective-permute-done | bytes 983072 | tf_op jit(solution)/shard_map/ppermute | solution.py:360
  61.0 32.0 %collective-permute-done = bf16[320,1536]{1,0:T(8,128)(2,1)} collective-permute-done((bf16[320,1536]{1,0:T(8,128)(2,1)}, bf16[320,1536]{1,0:T(8,128)(2,1)}, u32[]{:S(2)}, u32[]{:S(2)}) %collective-permute-start) | collective-permute-done | bytes 983072 | tf_op jit(solution)/shard_map/ppermute | solution.py:360
  93.0 0.0 all-gather.7.cloned.1.call-update
  93.1 0.0 all-gather.9.cloned.1.call-start
  93.1 0.7 all-gather.9.cloned.1.call-update
  93.8 0.0 all-gather.11.cloned.1.call-start
  93.8 0.5 all-gather.11.cloned.1.call-update
  94.4 9.6 %collective-permute-start.5 = (bf16[128,5120]{1,0:T(8,128)(2,1)}, bf16[128,5120]{1,0:T(8,128)(2,1)S(1)}, u32[]{:S(2)}, u32[]{:S(2)}) collective-permute-start(bf16[128,5120]{1,0:T(8,128)(2,1)} %get-tuple-element.30), channel_id=1, source_target_pairs={{0,1},{1,0},{2,3},{3,2},{4,5},{5,4},{6,7},{7,6},{8,9},{9,8},{10,11... | collective-permute-start | bytes 3932168 | tf_op jit(solution)/shard_map/ppermute | solution.py:360
  104.0 0.7 collective-permute-start.4
  104.7 27.4 %collective-permute-done.5.refs_2_.refs_6_ = bf16[128,5120]{1,0:T(8,128)(2,1)S(1)} collective-permute-done((bf16[128,5120]{1,0:T(8,128)(2,1)}, bf16[128,5120]{1,0:T(8,128)(2,1)S(1)}, u32[]{:S(2)}, u32[]{:S(2)}) %collective-permute-start.5) | collective-permute-done | bytes 1310752 | tf_op jit(solution)/shard_map/ppermute | solution.py:360
  132.1 1.1 copy-done.7
  133.2 1.8 collective-permute-start.6
  135.0 3.1 %collective-permute-start.7 = (bf16[64,5120]{1,0:T(8,128)(2,1)}, bf16[64,5120]{1,0:T(8,128)(2,1)S(1)}, u32[]{:S(2)}, u32[]{:S(2)}) collective-permute-start(bf16[64,5120]{1,0:T(8,128)(2,1)} %get-tuple-element.33), channel_id=1, source_target_pairs={{0,1},{1,0},{2,3},{3,2},{4,5},{5,4},{6,7},{7,6},{8,9},{9,8},{10,11... | collective-permute-start | bytes 1966088 | tf_op jit(solution)/shard_map/ppermute | solution.py:360
  138.1 1.3 collective-permute-start.9
  139.3 14.6 %collective-permute-done.7.refs_3_.refs_7_ = bf16[64,5120]{1,0:T(8,128)(2,1)S(1)} collective-permute-done((bf16[64,5120]{1,0:T(8,128)(2,1)}, bf16[64,5120]{1,0:T(8,128)(2,1)S(1)}, u32[]{:S(2)}, u32[]{:S(2)}) %collective-permute-start.7) | collective-permute-done | bytes 655392 | tf_op jit(solution)/shard_map/ppermute | solution.py:360
  153.9 0.9 copy-done.9
  154.8 15.1 %collective-permute-start.8 = (bf16[128,5120]{1,0:T(8,128)(2,1)}, bf16[128,5120]{1,0:T(8,128)(2,1)}, u32[]{:S(2)}, u32[]{:S(2)}) collective-permute-start(bf16[128,5120]{1,0:T(8,128)(2,1)} %get-tuple-element.34), channel_id=1, source_target_pairs={{0,2},{3,1},{4,6},{7,5},{8,10},{11,9},{12,14},{15,13},{16,18},{19,... | collective-permute-start | bytes 3932168 | tf_op jit(solution)/shard_map/ppermute | solution.py:360
  169.9 1.3 collective-permute-start.10
  171.1 10.9 %collective-permute-done.9.refs_2_ = bf16[128,5120]{1,0:T(8,128)(2,1)S(1)} collective-permute-done((bf16[128,5120]{1,0:T(8,128)(2,1)S(1)}, bf16[128,5120]{1,0:T(8,128)(2,1)S(1)}, u32[]{:S(2)}, u32[]{:S(2)}) %collective-permute-start.9) | collective-permute-done | bytes 1310752 | tf_op jit(solution)/shard_map/ppermute | solution.py:360
  182.0 1.1 copy-done.4
  183.1 11.7 %collective-permute-done.8.refs_0_ = bf16[128,5120]{1,0:T(8,128)(2,1)} collective-permute-done((bf16[128,5120]{1,0:T(8,128)(2,1)}, bf16[128,5120]{1,0:T(8,128)(2,1)}, u32[]{:S(2)}, u32[]{:S(2)}) %collective-permute-start.8) | collective-permute-done | bytes 1310752 | tf_op jit(solution)/shard_map/ppermute | solution.py:360
  194.8 6.3 %collective-permute-start.12 = (bf16[128,5120]{1,0:T(8,128)(2,1)}, bf16[128,5120]{1,0:T(8,128)(2,1)}, u32[]{:S(2)}, u32[]{:S(2)}) collective-permute-start(bf16[128,5120]{1,0:T(8,128)(2,1)} %get-tuple-element.46), channel_id=1, source_target_pairs={{0,2},{3,1},{4,6},{7,5},{8,10},{11,9},{12,14},{15,13},{16,18},{19,... | collective-permute-start | bytes 3932168 | tf_op jit(solution)/shard_map/ppermute | solution.py:360
  201.2 0.1 concatenate.21.scal
  201.3 1.3 collective-permute-start.11
  202.6 0.0 all-gather.5.cloned.1.call-done.refs_8_.refs_4_
  202.6 0.0 all-gather.7.cloned.1.call-done.refs_9_.refs_5_
  202.6 0.0 all-gather.9.cloned.1.call-done.refs_10_.refs_6_
  202.7 1.7 all-gather.11.cloned.1.call-done.refs_11_.refs_7_
  204.3 1.3 copy-done.8
  205.6 1.1 copy-done.10
  206.7 16.4 %project.3.refs_0_ = bf16[512,1536]{1,0:T(8,128)(2,1)} custom-call(s32[13]{0:T(128)S(1)} %concatenate.21.scal, bf16[256,5120]{1,0:T(8,128)(2,1)} %copy-done.12, bf16[64,5120]{1,0:T(8,128)(2,1)S(1)} %collective-permute-done.3.refs_1_.refs_5_, bf16[128,5120]{1,0:T(8,128)(2,1)S(1)} %copy-done.8, bf16[64,5120]{1,0:T(8,128)(2,1)S(1)} %copy-done.10, ...), custom_call_target="tpu_custom_call" | custom-call | flops 8053063680 | bytes 22544384 | tf_op jit(solution)/shard_map/project/pallas_call | solution.py:158
  223.2 2.0 collective-permute-done.12.refs_1_
  225.2 1.3 collective-permute-start.13
  227.2 0.1 concatenate.18.scal
  227.3 0.1 concatenate.22.scal
  227.4 0.1 stack.95.scal
  227.5 0.1 pad_add_fusion.scal
  227.5 1.3 copy-done.5
  228.9 12.2 %project.4.refs_1_ = bf16[256,1536]{1,0:T(8,128)(2,1)} custom-call(s32[11]{0:T(128)S(1)} %concatenate.22.scal, bf16[128,5120]{1,0:T(8,128)(2,1)S(1)} %collective-permute-done.4.refs_0_, bf16[128,5120]{1,0:T(8,128)(2,1)} %collective-permute-done.6.refs_1_, bf16[128,5120]{1,0:T(8,128)(2,1)S(1)} %copy-done.5, ...), custom_call_target="tpu_custom_call" | custom-call | flops 4026531840 | bytes 19136512 | tf_op jit(solution)/shard_map/project/pallas_call | solution.py:158
  241.1 1.3 copy-done.6
  242.3 1.5 copy-done.11
  243.9 10.2 %attend_near.1 = (f32[768,1024]{1,0:T(8,128)S(1)}, f32[768,128]{1,0:T(8,128)S(1)}, bf16[768,1536]{1,0:T(8,128)(2,1)S(1)}) custom-call(s32[7]{0:T(128)S(1)} %stack.95.scal, bf16[512,1536]{1,0:T(8,128)(2,1)S(1)} %copy-done.11, bf16[256,1536]{1,0:T(8,128)(2,1)S(1)} %copy-done.6), custom_call_target="tpu_custom_call" | custom-call | flops 1207959552 | bytes 3145728 | tf_op jit(solution)/shard_map/attend_near/pallas_call | solution.py:310
  254.1 9.7 %collective-permute-done.13.refs_3_ = bf16[128,5120]{1,0:T(8,128)(2,1)} collective-permute-done((bf16[128,5120]{1,0:T(8,128)(2,1)}, bf16[128,5120]{1,0:T(8,128)(2,1)}, u32[]{:S(2)}, u32[]{:S(2)}) %collective-permute-start.13) | collective-permute-done | bytes 1310752 | tf_op jit(solution)/shard_map/ppermute | solution.py:360
  263.8 2.1 copy-done.3
  265.9 9.0 %project.5.far = bf16[256,1536]{1,0:T(8,128)(2,1)S(1)} custom-call(s32[11]{0:T(128)S(1)} %concatenate.18.scal, bf16[128,5120]{1,0:T(8,128)(2,1)} %collective-permute-done.8.refs_0_, bf16[128,5120]{1,0:T(8,128)(2,1)} %collective-permute-done.12.refs_1_, bf16[128,5120]{1,0:T(8,128)(2,1)} %collective-permute-done.11.refs_2_, ...), custom_call_target="tpu_custom_call" | custom-call | flops 4026531840 | bytes 19136512 | tf_op jit(solution)/shard_map/project/pallas_call | solution.py:158
  275.0 10.9 %attend_far.1 = bf16[1024,1024]{1,0:T(8,128)(2,1)} custom-call(s32[2]{0:T(128)S(1)} %pad_add_fusion.scal, bf16[256,1536]{1,0:T(8,128)(2,1)S(1)} %project.5.far, bf16[768,1536]{1,0:T(8,128)(2,1)S(1)} %get-tuple-element.44.held, f32[768,1024]{1,0:T(8,128)S(1)} %get-tuple-element.42.partial, f32[768,128]{1,0:T(8,128)S(1)} %get-tuple-element.43.stats), custom_call_target="tpu_custom_call" | custom-call | flops 2147483648 | bytes 4194304 | tf_op jit(solution)/shard_map/attend_far/pallas_call | solution.py:332
  (33 shorter events, 0.1 us)
Async XLA Ops:
  6.5 196.1 %all-gather.5.cloned.1.call-start = ((), (), s32[]{:S(2)}) async-start(), calls=%async_computation | async-start | bytes 4915200 | tf_op jit(solution)/shard_map/all_gather | solution.py:366
  6.5 4.3 %copy-start.13 = (bf16[256,5120]{1,0:T(8,128)(2,1)S(1)}, bf16[256,5120]{1,0:T(8,128)(2,1)}, u32[]{:S(2)}) copy-start(bf16[256,5120]{1,0:T(8,128)(2,1)} %param.6) | copy-start | bytes 7864324
  10.8 0.7 copy-start.15
  10.8 191.8 %all-gather.7.cloned.1.call-start = ((), (), s32[]{:S(2)}) async-start(), calls=%async_computation.1 | async-start | bytes 4915200 | tf_op jit(solution)/shard_map/all_gather | solution.py:366
  12.3 8.3 %copy-start.12 = (bf16[256,5120]{1,0:T(8,128)(2,1)}, bf16[256,5120]{1,0:T(8,128)(2,1)S(1)}, u32[]{:S(2)}) copy-start(bf16[256,5120]{1,0:T(8,128)(2,1)S(1)} %fusion.2.refs_0_.refs_4_) | copy-start | bytes 7864324
  12.3 1.9 copy-start.14
  13.2 29.6 %collective-permute-start.3 = (bf16[64,5120]{1,0:T(8,128)(2,1)S(1)}, bf16[64,5120]{1,0:T(8,128)(2,1)S(1)}, u32[]{:S(2)}, u32[]{:S(2)}) collective-permute-start(bf16[64,5120]{1,0:T(8,128)(2,1)S(1)} %get-tuple-element.56), channel_id=1, source_target_pairs={{0,1},{1,0},{2,3},{3,2},{4,5},{5,4},{6,7},{7,6},{8,9},{9,8},{10,11... | collective-permute-start | bytes 1966088 | tf_op jit(solution)/shard_map/ppermute | solution.py:360
  14.2 46.8 %collective-permute-start.1 = (bf16[320,1536]{1,0:T(8,128)(2,1)S(1)}, bf16[320,1536]{1,0:T(8,128)(2,1)}, u32[]{:S(2)}, u32[]{:S(2)}) collective-permute-start(bf16[320,1536]{1,0:T(8,128)(2,1)S(1)} %copy-done.14), channel_id=1, source_target_pairs={{0,2},{1,3},{2,0},{3,1},{4,6},{5,7},{6,4},{7,5},{8,10},{9,11},{10,... | collective-permute-start | bytes 2949128 | tf_op jit(solution)/shard_map/ppermute | solution.py:360
  14.6 78.5 %collective-permute-start = (bf16[320,1536]{1,0:T(8,128)(2,1)}, bf16[320,1536]{1,0:T(8,128)(2,1)}, u32[]{:S(2)}, u32[]{:S(2)}) collective-permute-start(bf16[320,1536]{1,0:T(8,128)(2,1)} %get-tuple-element.53), channel_id=1, source_target_pairs={{0,1},{1,0},{2,3},{3,2},{4,5},{5,4},{6,7},{7,6},{8,9},{9,8},{10,11... | collective-permute-start | bytes 2949128 | tf_op jit(solution)/shard_map/ppermute | solution.py:360
  15.6 77.4 %collective-permute-start.2 = (bf16[320,1536]{1,0:T(8,128)(2,1)}, bf16[320,1536]{1,0:T(8,128)(2,1)}, u32[]{:S(2)}, u32[]{:S(2)}) collective-permute-start(bf16[320,1536]{1,0:T(8,128)(2,1)} %get-tuple-element.54), channel_id=1, source_target_pairs={{0,3},{1,2},{2,1},{3,0},{4,7},{5,6},{6,5},{7,4},{8,11},{9,10},{10,... | collective-permute-start | bytes 2949128 | tf_op jit(solution)/shard_map/ppermute | solution.py:360
  22.6 178.7 %copy-start.16 = (f32[128]{0:T(128)S(1)}, f32[128]{0:T(128)}, u32[]{:S(2)}) copy-start(f32[128]{0:T(128)} %param.10) | copy-start | bytes 1540
  22.6 178.7 %copy-start.17 = (f32[128]{0:T(128)S(1)}, f32[128]{0:T(128)}, u32[]{:S(2)}) copy-start(f32[128]{0:T(128)} %param.9) | copy-start | bytes 1540
  93.1 109.6 %all-gather.9.cloned.1.call-start = ((), (), s32[]{:S(2)}) async-start(), calls=%async_computation.2 | async-start | bytes 4915200 | tf_op jit(solution)/shard_map/all_gather | solution.py:366
  93.8 110.5 %all-gather.11.cloned.1.call-start = ((), (), s32[]{:S(2)}) async-start(), calls=%async_computation.3 | async-start | bytes 4915200 | tf_op jit(solution)/shard_map/all_gather | solution.py:366
  94.4 37.8 %collective-permute-start.5 = (bf16[128,5120]{1,0:T(8,128)(2,1)}, bf16[128,5120]{1,0:T(8,128)(2,1)S(1)}, u32[]{:S(2)}, u32[]{:S(2)}) collective-permute-start(bf16[128,5120]{1,0:T(8,128)(2,1)} %get-tuple-element.30), channel_id=1, source_target_pairs={{0,1},{1,0},{2,3},{3,2},{4,5},{5,4},{6,7},{7,6},{8,9},{9,8},{10,11... | collective-permute-start | bytes 3932168 | tf_op jit(solution)/shard_map/ppermute | solution.py:360
  104.0 29.2 %collective-permute-start.4 = (bf16[128,5120]{1,0:T(8,128)(2,1)}, bf16[128,5120]{1,0:T(8,128)(2,1)S(1)}, u32[]{:S(2)}, u32[]{:S(2)}) collective-permute-start(bf16[128,5120]{1,0:T(8,128)(2,1)} %get-tuple-element.34), channel_id=1, source_target_pairs={{1,2},{2,1},{5,6},{6,5},{9,10},{10,9},{13,14},{14,13},{17,18},{18,... | collective-permute-start | bytes 3932168 | tf_op jit(solution)/shard_map/ppermute | solution.py:360
  132.1 1.1 copy-start.7
  133.2 21.6 %collective-permute-start.6 = (bf16[128,5120]{1,0:T(8,128)(2,1)}, bf16[128,5120]{1,0:T(8,128)(2,1)}, u32[]{:S(2)}, u32[]{:S(2)}) collective-permute-start(bf16[128,5120]{1,0:T(8,128)(2,1)} %get-tuple-element.46), channel_id=1, source_target_pairs={{1,2},{2,1},{5,6},{6,5},{9,10},{10,9},{13,14},{14,13},{17,18},{18,... | collective-permute-start | bytes 3932168 | tf_op jit(solution)/shard_map/ppermute | solution.py:360
  135.0 19.0 %collective-permute-start.7 = (bf16[64,5120]{1,0:T(8,128)(2,1)}, bf16[64,5120]{1,0:T(8,128)(2,1)S(1)}, u32[]{:S(2)}, u32[]{:S(2)}) collective-permute-start(bf16[64,5120]{1,0:T(8,128)(2,1)} %get-tuple-element.33), channel_id=1, source_target_pairs={{0,1},{1,0},{2,3},{3,2},{4,5},{5,4},{6,7},{7,6},{8,9},{9,8},{10,11... | collective-permute-start | bytes 1966088 | tf_op jit(solution)/shard_map/ppermute | solution.py:360
  138.1 43.9 %collective-permute-start.9 = (bf16[128,5120]{1,0:T(8,128)(2,1)S(1)}, bf16[128,5120]{1,0:T(8,128)(2,1)S(1)}, u32[]{:S(2)}, u32[]{:S(2)}) collective-permute-start(bf16[128,5120]{1,0:T(8,128)(2,1)S(1)} %collective-permute-done.4.refs_0_), channel_id=1, source_target_pairs={{1,0},{2,3},{5,4},{6,7},{9,8},{10,11},{13,12},{14,15},{17,16},{18,... | collective-permute-start | bytes 3932168 | tf_op jit(solution)/shard_map/ppermute | solution.py:360
  153.9 0.9 copy-start.9
  154.8 40.0 %collective-permute-start.8 = (bf16[128,5120]{1,0:T(8,128)(2,1)}, bf16[128,5120]{1,0:T(8,128)(2,1)}, u32[]{:S(2)}, u32[]{:S(2)}) collective-permute-start(bf16[128,5120]{1,0:T(8,128)(2,1)} %get-tuple-element.34), channel_id=1, source_target_pairs={{0,2},{3,1},{4,6},{7,5},{8,10},{11,9},{12,14},{15,13},{16,18},{19,... | collective-permute-start | bytes 3932168 | tf_op jit(solution)/shard_map/ppermute | solution.py:360
  169.9 53.3 %collective-permute-start.10 = (bf16[128,5120]{1,0:T(8,128)(2,1)}, bf16[128,5120]{1,0:T(8,128)(2,1)}, u32[]{:S(2)}, u32[]{:S(2)}) collective-permute-start(bf16[128,5120]{1,0:T(8,128)(2,1)} %collective-permute-done.6.refs_1_), channel_id=1, source_target_pairs={{1,0},{2,3},{5,4},{6,7},{9,8},{10,11},{13,12},{14,15},{17,16},{18,... | collective-permute-start | bytes 3932168 | tf_op jit(solution)/shard_map/ppermute | solution.py:360
  182.0 1.1 copy-start.4
  194.8 30.4 %collective-permute-start.12 = (bf16[128,5120]{1,0:T(8,128)(2,1)}, bf16[128,5120]{1,0:T(8,128)(2,1)}, u32[]{:S(2)}, u32[]{:S(2)}) collective-permute-start(bf16[128,5120]{1,0:T(8,128)(2,1)} %get-tuple-element.46), channel_id=1, source_target_pairs={{0,2},{3,1},{4,6},{7,5},{8,10},{11,9},{12,14},{15,13},{16,18},{19,... | collective-permute-start | bytes 3932168 | tf_op jit(solution)/shard_map/ppermute | solution.py:360
  201.3 39.8 %collective-permute-start.11 = (bf16[128,5120]{1,0:T(8,128)(2,1)}, bf16[128,5120]{1,0:T(8,128)(2,1)}, u32[]{:S(2)}, u32[]{:S(2)}) collective-permute-start(bf16[128,5120]{1,0:T(8,128)(2,1)} %collective-permute-done.8.refs_0_), channel_id=1, source_target_pairs={{1,0},{2,3},{5,4},{6,7},{9,8},{10,11},{13,12},{14,15},{17,16},{18,... | collective-permute-start | bytes 3932168 | tf_op jit(solution)/shard_map/ppermute | solution.py:360
  204.3 1.3 copy-start.8
  205.6 1.1 copy-start.10
  225.2 38.6 %collective-permute-start.13 = (bf16[128,5120]{1,0:T(8,128)(2,1)}, bf16[128,5120]{1,0:T(8,128)(2,1)}, u32[]{:S(2)}, u32[]{:S(2)}) collective-permute-start(bf16[128,5120]{1,0:T(8,128)(2,1)} %collective-permute-done.12.refs_1_), channel_id=1, source_target_pairs={{1,0},{2,3},{5,4},{6,7},{9,8},{10,11},{13,12},{14,15},{17,16},{18,... | collective-permute-start | bytes 3932168 | tf_op jit(solution)/shard_map/ppermute | solution.py:360
  227.5 1.3 copy-start.5
  228.9 35.0 %copy-start.1 = (bf16[1280,1536]{1,0:T(8,128)(2,1)S(1)}, bf16[1280,1536]{1,0:T(8,128)(2,1)}, u32[]{:S(2)}) copy-start(bf16[1280,1536]{1,0:T(8,128)(2,1)} %all-gather.7.cloned.1.call-done.refs_9_.refs_5_) | copy-start | bytes 11796484
  228.9 35.0 %copy-start.2 = (bf16[1280,1536]{1,0:T(8,128)(2,1)S(1)}, bf16[1280,1536]{1,0:T(8,128)(2,1)}, u32[]{:S(2)}) copy-start(bf16[1280,1536]{1,0:T(8,128)(2,1)} %all-gather.9.cloned.1.call-done.refs_10_.refs_6_) | copy-start | bytes 11796484
  241.0 22.8 %copy-start = (bf16[1280,1536]{1,0:T(8,128)(2,1)S(1)}, bf16[1280,1536]{1,0:T(8,128)(2,1)}, u32[]{:S(2)}) copy-start(bf16[1280,1536]{1,0:T(8,128)(2,1)} %all-gather.5.cloned.1.call-done.refs_8_.refs_4_) | copy-start | bytes 11796484
  241.1 1.3 copy-start.6
  242.3 1.5 copy-start.11
  263.8 2.1 copy-start.3
Sparse Core Ops, SparseCore 0:
  10.9 33.9 all-gather.4
  93.2 42.0 all-gather.6
  136.8 32.9 all-gather.8
  171.3 32.9 all-gather.10

commit v3 on v2

--- a/solution.py
+++ b/solution.py
@@ -370,7 +370,10 @@
     outward = [(1, 0), (2, 3)]
 
     planes = [t] + [jnp.bitwise_xor(t, m) for m in (1, 2, 3)]
-    own, out1, out2, out3 = [slab(p) for p in planes]
+    out2 = slab(planes[2])
+    w_qkv = after(w_qkv, out2)
+    own, out1, out3 = [slab(p) for p in (planes[0], planes[1], planes[3])]
+    tokens = after(tokens, out1)
     normed = head_norm(tokens.astype(jnp.float32), norm_gain).astype(jnp.bfloat16)
     first, second = normed[:half], normed[half:]
 

time: 298 us -> 298 us (level)
    unnamed x36 -> x34, local copies, waits for them, and re-layouts: 12.3 us -> 11.7 us
  transfers between devices with their start and end apart: 18 -> 18, of which waited for: 10 -> 7; matrix products, arithmetic and copies ran while one was open for 2% -> 2% of each run, Pallas kernels for 13% -> 13%
where the time goes in v3:
time: 298 us; the launch traced here: 293 us
  waiting for transfers between devices  151 us (51%)
  Pallas kernels  58.8 us (20%)
  starting transfers between devices  44.6 us (15%)
  local copies, waits for them, and re-layouts  21 us (7%)
  between operations  14.5 us (5%)
  other arithmetic  3.71 us (1%)
    ppermute x14, waiting for transfers between devices, across(): return lax.ppermute(x, 'tensor', pairs)  149 us
    ppermute x14, starting transfers between devices, across(): return lax.ppermute(x, 'tensor', pairs)  44.5 us
    pallas_call x3, Pallas kernels, project(): pl.pallas_call(functools.partial(project_kernel, counts, sources, tile),...  37.7 us
    unnamed x34, local copies, waits for them, and re-layouts  11.7 us
    pallas_call x1, Pallas kernels, attend_far(): pl.pallas_call(attend_far_kernel, out_shape=jax.ShapeDtypeStruct((rows, w...  10.9 us
    pallas_call x1, Pallas kernels, attend_near(): pl.pallas_call(functools.partial(attend_near_kernel, parts, block), out_s...  10.2 us
  transfers between devices with their start and end apart: 18, of which 7 were waited for; matrix products, arithmetic and copies ran while one was open for 2% of the time, Pallas kernels for 13%

profile of v3, /device:TPU:24, one launch (start us, length us, event | category | flops | bytes accessed | tf_op | source)
XLA Modules:
  0.0 293.2 jit_solution(11874528567929331719)
XLA Ops:
  6.5 2.2 constant_dynamic-slice_fusion.3
  8.8 3.6 %constant_dynamic-slice_fusion = (bf16[320,1536]{1,0:T(8,128)(2,1)}, bf16[320,1536]{1,0:T(8,128)(2,1)}, bf16[320,1536]{1,0:T(8,128)(2,1)}) fusion(bf16[320,6144]{1,0:T(8,128)(2,1)} %param.7, s32[]{:T(128)S(6)} %select_n.26, s32[]{:T(128)S(6)} %select_n.25, s32[]{:T(128)S(6)} %select_n.24), kind=kLoop, calls=%fused_computation.13 | loop fusion | bytes 5898252 | tf_op jit(solution)/shard_map/dynamic_slice | solution.py:357
  12.4 0.0 all-gather.5.cloned.1.call-update
  12.4 0.0 all-gather.7.cloned.1.call-start
  12.5 0.4 collective-permute-start.1
  12.9 2.5 collective-permute-start.2
  15.3 0.7 collective-permute-start
  16.0 0.6 fusion
  16.6 0.8 fusion.2.refs_0_.refs_4_
  17.4 1.1 fusion.4
  18.5 1.3 collective-permute-start.3
  19.8 2.0 fusion.5
  21.9 1.9 fusion.3
  23.8 0.0 copy-start.15
  23.8 0.0 copy-start.16
  23.8 0.3 pad_maximum_fusion
  24.1 70.4 %collective-permute-done.3.refs_1_.refs_5_ = bf16[64,5120]{1,0:T(8,128)(2,1)S(1)} collective-permute-done((bf16[64,5120]{1,0:T(8,128)(2,1)S(1)}, bf16[64,5120]{1,0:T(8,128)(2,1)S(1)}, u32[]{:S(2)}, u32[]{:S(2)}) %collective-permute-start.3) | collective-permute-done | bytes 655392 | tf_op jit(solution)/shard_map/ppermute | solution.py:360
  94.6 0.0 collective-permute-done.1
  94.6 0.0 collective-permute-done.2
  94.6 0.0 all-gather.7.cloned.1.call-update
  94.6 0.0 all-gather.9.cloned.1.call-start
  94.6 0.7 all-gather.9.cloned.1.call-update
  95.3 0.0 all-gather.11.cloned.1.call-start
  95.4 0.5 all-gather.11.cloned.1.call-update
  95.9 6.4 %collective-permute-start.5 = (bf16[128,5120]{1,0:T(8,128)(2,1)}, bf16[128,5120]{1,0:T(8,128)(2,1)S(1)}, u32[]{:S(2)}, u32[]{:S(2)}) collective-permute-start(bf16[128,5120]{1,0:T(8,128)(2,1)} %get-tuple-element.34), channel_id=1, source_target_pairs={{0,1},{1,0},{2,3},{3,2},{4,5},{5,4},{6,7},{7,6},{8,9},{9,8},{10,11... | collective-permute-start | bytes 3932168 | tf_op jit(solution)/shard_map/ppermute | solution.py:360
  102.3 0.7 collective-permute-start.4
  103.1 28.4 %collective-permute-done.5.refs_2_.refs_6_ = bf16[128,5120]{1,0:T(8,128)(2,1)S(1)} collective-permute-done((bf16[128,5120]{1,0:T(8,128)(2,1)}, bf16[128,5120]{1,0:T(8,128)(2,1)S(1)}, u32[]{:S(2)}, u32[]{:S(2)}) %collective-permute-start.5) | collective-permute-done | bytes 1310752 | tf_op jit(solution)/shard_map/ppermute | solution.py:360
  131.5 1.1 copy-done.7
  132.6 1.7 collective-permute-start.6
  134.3 3.1 %collective-permute-start.7 = (bf16[64,5120]{1,0:T(8,128)(2,1)}, bf16[64,5120]{1,0:T(8,128)(2,1)S(1)}, u32[]{:S(2)}, u32[]{:S(2)}) collective-permute-start(bf16[64,5120]{1,0:T(8,128)(2,1)} %get-tuple-element.37), channel_id=1, source_target_pairs={{0,1},{1,0},{2,3},{3,2},{4,5},{5,4},{6,7},{7,6},{8,9},{9,8},{10,11... | collective-permute-start | bytes 1966088 | tf_op jit(solution)/shard_map/ppermute | solution.py:360
  137.4 1.3 collective-permute-start.9
  138.7 14.6 %collective-permute-done.7.refs_3_.refs_7_ = bf16[64,5120]{1,0:T(8,128)(2,1)S(1)} collective-permute-done((bf16[64,5120]{1,0:T(8,128)(2,1)}, bf16[64,5120]{1,0:T(8,128)(2,1)S(1)}, u32[]{:S(2)}, u32[]{:S(2)}) %collective-permute-start.7) | collective-permute-done | bytes 655392 | tf_op jit(solution)/shard_map/ppermute | solution.py:360
  153.3 0.9 copy-done.9
  154.1 16.1 %collective-permute-start.8 = (bf16[128,5120]{1,0:T(8,128)(2,1)}, bf16[128,5120]{1,0:T(8,128)(2,1)}, u32[]{:S(2)}, u32[]{:S(2)}) collective-permute-start(bf16[128,5120]{1,0:T(8,128)(2,1)} %get-tuple-element.38), channel_id=1, source_target_pairs={{0,2},{3,1},{4,6},{7,5},{8,10},{11,9},{12,14},{15,13},{16,18},{19,... | collective-permute-start | bytes 3932168 | tf_op jit(solution)/shard_map/ppermute | solution.py:360
  170.2 1.3 collective-permute-start.10
  171.5 9.9 %collective-permute-done.9.refs_2_ = bf16[128,5120]{1,0:T(8,128)(2,1)S(1)} collective-permute-done((bf16[128,5120]{1,0:T(8,128)(2,1)S(1)}, bf16[128,5120]{1,0:T(8,128)(2,1)S(1)}, u32[]{:S(2)}, u32[]{:S(2)}) %collective-permute-start.9) | collective-permute-done | bytes 1310752 | tf_op jit(solution)/shard_map/ppermute | solution.py:360
  181.4 1.1 copy-done.4
  182.5 13.7 %collective-permute-done.8.refs_0_ = bf16[128,5120]{1,0:T(8,128)(2,1)} collective-permute-done((bf16[128,5120]{1,0:T(8,128)(2,1)}, bf16[128,5120]{1,0:T(8,128)(2,1)}, u32[]{:S(2)}, u32[]{:S(2)}) %collective-permute-start.8) | collective-permute-done | bytes 1310752 | tf_op jit(solution)/shard_map/ppermute | solution.py:360
  196.2 6.4 %collective-permute-start.12 = (bf16[128,5120]{1,0:T(8,128)(2,1)}, bf16[128,5120]{1,0:T(8,128)(2,1)}, u32[]{:S(2)}, u32[]{:S(2)}) collective-permute-start(bf16[128,5120]{1,0:T(8,128)(2,1)} %get-tuple-element.50), channel_id=1, source_target_pairs={{0,2},{3,1},{4,6},{7,5},{8,10},{11,9},{12,14},{15,13},{16,18},{19,... | collective-permute-start | bytes 3932168 | tf_op jit(solution)/shard_map/ppermute | solution.py:360
  202.6 0.1 concatenate.21.scal
  202.7 1.3 collective-permute-start.11
  204.0 0.0 all-gather.5.cloned.1.call-done.refs_8_.refs_4_
  204.0 0.0 all-gather.7.cloned.1.call-done.refs_9_.refs_5_
  204.0 0.0 all-gather.9.cloned.1.call-done.refs_10_.refs_6_
  204.1 0.0 all-gather.11.cloned.1.call-done.refs_11_.refs_7_
  204.1 0.0 copy-start.8
  204.1 1.3 copy-done.8
  205.4 1.1 copy-done.10
  206.5 16.4 %project.3.refs_0_ = bf16[512,1536]{1,0:T(8,128)(2,1)} custom-call(s32[13]{0:T(128)S(1)} %concatenate.21.scal, bf16[256,5120]{1,0:T(8,128)(2,1)} %copy-done.12, bf16[64,5120]{1,0:T(8,128)(2,1)S(1)} %collective-permute-done.3.refs_1_.refs_5_, bf16[128,5120]{1,0:T(8,128)(2,1)S(1)} %copy-done.8, bf16[64,5120]{1,0:T(8,128)(2,1)S(1)} %copy-done.10, ...), custom_call_target="tpu_custom_call" | custom-call | flops 8053063680 | bytes 22544384 | tf_op jit(solution)/shard_map/project/pallas_call | solution.py:158
  223.0 4.7 %collective-permute-done.12.refs_1_ = bf16[128,5120]{1,0:T(8,128)(2,1)} collective-permute-done((bf16[128,5120]{1,0:T(8,128)(2,1)}, bf16[128,5120]{1,0:T(8,128)(2,1)}, u32[]{:S(2)}, u32[]{:S(2)}) %collective-permute-start.12) | collective-permute-done | bytes 1310752 | tf_op jit(solution)/shard_map/ppermute | solution.py:360
  227.6 1.3 collective-permute-start.13
  229.6 0.1 concatenate.18.scal
  229.7 0.1 concatenate.22.scal
  229.8 0.1 stack.95.scal
  229.9 0.1 pad_add_fusion.scal
  229.9 1.3 copy-done.5
  231.3 12.2 %project.4.refs_1_ = bf16[256,1536]{1,0:T(8,128)(2,1)} custom-call(s32[11]{0:T(128)S(1)} %concatenate.22.scal, bf16[128,5120]{1,0:T(8,128)(2,1)S(1)} %collective-permute-done.4.refs_0_, bf16[128,5120]{1,0:T(8,128)(2,1)} %collective-permute-done.6.refs_1_, bf16[128,5120]{1,0:T(8,128)(2,1)S(1)} %copy-done.5, ...), custom_call_target="tpu_custom_call" | custom-call | flops 4026531840 | bytes 19136512 | tf_op jit(solution)/shard_map/project/pallas_call | solution.py:158
  243.5 1.3 copy-done.6
  244.8 1.5 copy-done.11
  246.3 10.2 %attend_near.1 = (f32[768,1024]{1,0:T(8,128)S(1)}, f32[768,128]{1,0:T(8,128)S(1)}, bf16[768,1536]{1,0:T(8,128)(2,1)S(1)}) custom-call(s32[7]{0:T(128)S(1)} %stack.95.scal, bf16[512,1536]{1,0:T(8,128)(2,1)S(1)} %copy-done.11, bf16[256,1536]{1,0:T(8,128)(2,1)S(1)} %copy-done.6), custom_call_target="tpu_custom_call" | custom-call | flops 1207959552 | bytes 3145728 | tf_op jit(solution)/shard_map/attend_near/pallas_call | solution.py:310
  256.6 7.6 %collective-permute-done.13.refs_3_ = bf16[128,5120]{1,0:T(8,128)(2,1)} collective-permute-done((bf16[128,5120]{1,0:T(8,128)(2,1)}, bf16[128,5120]{1,0:T(8,128)(2,1)}, u32[]{:S(2)}, u32[]{:S(2)}) %collective-permute-start.13) | collective-permute-done | bytes 1310752 | tf_op jit(solution)/shard_map/ppermute | solution.py:360
  264.2 2.1 copy-done.3
  266.3 9.0 %project.5.far = bf16[256,1536]{1,0:T(8,128)(2,1)S(1)} custom-call(s32[11]{0:T(128)S(1)} %concatenate.18.scal, bf16[128,5120]{1,0:T(8,128)(2,1)} %collective-permute-done.8.refs_0_, bf16[128,5120]{1,0:T(8,128)(2,1)} %collective-permute-done.12.refs_1_, bf16[128,5120]{1,0:T(8,128)(2,1)} %collective-permute-done.11.refs_2_, ...), custom_call_target="tpu_custom_call" | custom-call | flops 4026531840 | bytes 19136512 | tf_op jit(solution)/shard_map/project/pallas_call | solution.py:158
  275.4 10.9 %attend_far.1 = bf16[1024,1024]{1,0:T(8,128)(2,1)} custom-call(s32[2]{0:T(128)S(1)} %pad_add_fusion.scal, bf16[256,1536]{1,0:T(8,128)(2,1)S(1)} %project.5.far, bf16[768,1536]{1,0:T(8,128)(2,1)S(1)} %get-tuple-element.48.held, f32[768,1024]{1,0:T(8,128)S(1)} %get-tuple-element.46.partial, f32[768,128]{1,0:T(8,128)S(1)} %get-tuple-element.47.stats), custom_call_target="tpu_custom_call" | custom-call | flops 2147483648 | bytes 4194304 | tf_op jit(solution)/shard_map/attend_far/pallas_call | solution.py:332
  (32 shorter events, 0.1 us)
Async XLA Ops:
  6.5 197.5 %all-gather.5.cloned.1.call-start = ((), (), s32[]{:S(2)}) async-start(), calls=%async_computation | async-start | bytes 4915200 | tf_op jit(solution)/shard_map/all_gather | solution.py:366
  8.8 7.2 %copy-start.13 = (bf16[256,5120]{1,0:T(8,128)(2,1)S(1)}, bf16[256,5120]{1,0:T(8,128)(2,1)}, u32[]{:S(2)}) copy-start(bf16[256,5120]{1,0:T(8,128)(2,1)} %param.6) | copy-start | bytes 7864324
  12.4 4.2 %copy-start.14 = (f32[5120]{0:T(1024)S(1)}, f32[5120]{0:T(1024)}, u32[]{:S(2)}) copy-start(f32[5120]{0:T(1024)} %param.8) | copy-start | bytes 61444
  12.4 191.6 %all-gather.7.cloned.1.call-start = ((), (), s32[]{:S(2)}) async-start(), calls=%async_computation.1 | async-start | bytes 4915200 | tf_op jit(solution)/shard_map/all_gather | solution.py:366
  12.5 82.1 %collective-permute-start.1 = (bf16[320,1536]{1,0:T(8,128)(2,1)}, bf16[320,1536]{1,0:T(8,128)(2,1)}, u32[]{:S(2)}, u32[]{:S(2)}) collective-permute-start(bf16[320,1536]{1,0:T(8,128)(2,1)} %constant_dynamic-slice_fusion.3), channel_id=1, source_target_pairs={{0,2},{1,3},{2,0},{3,1},{4,6},{5,7},{6,4},{7,5},{8,10},{9,11},{10,... | collective-permute-start | bytes 2949128 | tf_op jit(solution)/shard_map/ppermute | solution.py:360
  12.9 81.7 %collective-permute-start.2 = (bf16[320,1536]{1,0:T(8,128)(2,1)}, bf16[320,1536]{1,0:T(8,128)(2,1)}, u32[]{:S(2)}, u32[]{:S(2)}) collective-permute-start(bf16[320,1536]{1,0:T(8,128)(2,1)} %get-tuple-element.56), channel_id=1, source_target_pairs={{0,3},{1,2},{2,1},{3,0},{4,7},{5,6},{6,5},{7,4},{8,11},{9,10},{10,... | collective-permute-start | bytes 2949128 | tf_op jit(solution)/shard_map/ppermute | solution.py:360
  15.3 79.2 %collective-permute-start = (bf16[320,1536]{1,0:T(8,128)(2,1)}, bf16[320,1536]{1,0:T(8,128)(2,1)}, u32[]{:S(2)}, u32[]{:S(2)}) collective-permute-start(bf16[320,1536]{1,0:T(8,128)(2,1)} %get-tuple-element.57), channel_id=1, source_target_pairs={{0,1},{1,0},{2,3},{3,2},{4,5},{5,4},{6,7},{7,6},{8,9},{9,8},{10,11... | collective-permute-start | bytes 2949128 | tf_op jit(solution)/shard_map/ppermute | solution.py:360
  17.4 4.4 %copy-start.12 = (bf16[256,5120]{1,0:T(8,128)(2,1)}, bf16[256,5120]{1,0:T(8,128)(2,1)S(1)}, u32[]{:S(2)}) copy-start(bf16[256,5120]{1,0:T(8,128)(2,1)S(1)} %fusion.2.refs_0_.refs_4_) | copy-start | bytes 7864324
  18.5 76.1 %collective-permute-start.3 = (bf16[64,5120]{1,0:T(8,128)(2,1)S(1)}, bf16[64,5120]{1,0:T(8,128)(2,1)S(1)}, u32[]{:S(2)}, u32[]{:S(2)}) collective-permute-start(bf16[64,5120]{1,0:T(8,128)(2,1)S(1)} %get-tuple-element.59), channel_id=1, source_target_pairs={{0,1},{1,0},{2,3},{3,2},{4,5},{5,4},{6,7},{7,6},{8,9},{9,8},{10,11... | collective-permute-start | bytes 1966088 | tf_op jit(solution)/shard_map/ppermute | solution.py:360
  23.8 178.9 %copy-start.15 = (f32[128]{0:T(128)S(1)}, f32[128]{0:T(128)}, u32[]{:S(2)}) copy-start(f32[128]{0:T(128)} %param.10) | copy-start | bytes 1540
  23.8 178.9 %copy-start.16 = (f32[128]{0:T(128)S(1)}, f32[128]{0:T(128)}, u32[]{:S(2)}) copy-start(f32[128]{0:T(128)} %param.9) | copy-start | bytes 1540
  94.6 109.5 %all-gather.9.cloned.1.call-start = ((), (), s32[]{:S(2)}) async-start(), calls=%async_computation.2 | async-start | bytes 4915200 | tf_op jit(solution)/shard_map/all_gather | solution.py:366
  95.3 108.8 %all-gather.11.cloned.1.call-start = ((), (), s32[]{:S(2)}) async-start(), calls=%async_computation.3 | async-start | bytes 4915200 | tf_op jit(solution)/shard_map/all_gather | solution.py:366
  95.9 35.6 %collective-permute-start.5 = (bf16[128,5120]{1,0:T(8,128)(2,1)}, bf16[128,5120]{1,0:T(8,128)(2,1)S(1)}, u32[]{:S(2)}, u32[]{:S(2)}) collective-permute-start(bf16[128,5120]{1,0:T(8,128)(2,1)} %get-tuple-element.34), channel_id=1, source_target_pairs={{0,1},{1,0},{2,3},{3,2},{4,5},{5,4},{6,7},{7,6},{8,9},{9,8},{10,11... | collective-permute-start | bytes 3932168 | tf_op jit(solution)/shard_map/ppermute | solution.py:360
  102.3 30.2 %collective-permute-start.4 = (bf16[128,5120]{1,0:T(8,128)(2,1)}, bf16[128,5120]{1,0:T(8,128)(2,1)S(1)}, u32[]{:S(2)}, u32[]{:S(2)}) collective-permute-start(bf16[128,5120]{1,0:T(8,128)(2,1)} %get-tuple-element.38), channel_id=1, source_target_pairs={{1,2},{2,1},{5,6},{6,5},{9,10},{10,9},{13,14},{14,13},{17,18},{18,... | collective-permute-start | bytes 3932168 | tf_op jit(solution)/shard_map/ppermute | solution.py:360
  131.5 1.1 copy-start.7
  132.6 21.6 %collective-permute-start.6 = (bf16[128,5120]{1,0:T(8,128)(2,1)}, bf16[128,5120]{1,0:T(8,128)(2,1)}, u32[]{:S(2)}, u32[]{:S(2)}) collective-permute-start(bf16[128,5120]{1,0:T(8,128)(2,1)} %get-tuple-element.50), channel_id=1, source_target_pairs={{1,2},{2,1},{5,6},{6,5},{9,10},{10,9},{13,14},{14,13},{17,18},{18,... | collective-permute-start | bytes 3932168 | tf_op jit(solution)/shard_map/ppermute | solution.py:360
  134.3 19.0 %collective-permute-start.7 = (bf16[64,5120]{1,0:T(8,128)(2,1)}, bf16[64,5120]{1,0:T(8,128)(2,1)S(1)}, u32[]{:S(2)}, u32[]{:S(2)}) collective-permute-start(bf16[64,5120]{1,0:T(8,128)(2,1)} %get-tuple-element.37), channel_id=1, source_target_pairs={{0,1},{1,0},{2,3},{3,2},{4,5},{5,4},{6,7},{7,6},{8,9},{9,8},{10,11... | collective-permute-start | bytes 1966088 | tf_op jit(solution)/shard_map/ppermute | solution.py:360
  137.4 43.9 %collective-permute-start.9 = (bf16[128,5120]{1,0:T(8,128)(2,1)S(1)}, bf16[128,5120]{1,0:T(8,128)(2,1)S(1)}, u32[]{:S(2)}, u32[]{:S(2)}) collective-permute-start(bf16[128,5120]{1,0:T(8,128)(2,1)S(1)} %collective-permute-done.4.refs_0_), channel_id=1, source_target_pairs={{1,0},{2,3},{5,4},{6,7},{9,8},{10,11},{13,12},{14,15},{17,16},{18,... | collective-permute-start | bytes 3932168 | tf_op jit(solution)/shard_map/ppermute | solution.py:360
  153.3 0.9 copy-start.9
  154.1 42.1 %collective-permute-start.8 = (bf16[128,5120]{1,0:T(8,128)(2,1)}, bf16[128,5120]{1,0:T(8,128)(2,1)}, u32[]{:S(2)}, u32[]{:S(2)}) collective-permute-start(bf16[128,5120]{1,0:T(8,128)(2,1)} %get-tuple-element.38), channel_id=1, source_target_pairs={{0,2},{3,1},{4,6},{7,5},{8,10},{11,9},{12,14},{15,13},{16,18},{19,... | collective-permute-start | bytes 3932168 | tf_op jit(solution)/shard_map/ppermute | solution.py:360
  170.2 52.7 %collective-permute-start.10 = (bf16[128,5120]{1,0:T(8,128)(2,1)}, bf16[128,5120]{1,0:T(8,128)(2,1)}, u32[]{:S(2)}, u32[]{:S(2)}) collective-permute-start(bf16[128,5120]{1,0:T(8,128)(2,1)} %collective-permute-done.6.refs_1_), channel_id=1, source_target_pairs={{1,0},{2,3},{5,4},{6,7},{9,8},{10,11},{13,12},{14,15},{17,16},{18,... | collective-permute-start | bytes 3932168 | tf_op jit(solution)/shard_map/ppermute | solution.py:360
  181.4 1.1 copy-start.4
  196.2 31.4 %collective-permute-start.12 = (bf16[128,5120]{1,0:T(8,128)(2,1)}, bf16[128,5120]{1,0:T(8,128)(2,1)}, u32[]{:S(2)}, u32[]{:S(2)}) collective-permute-start(bf16[128,5120]{1,0:T(8,128)(2,1)} %get-tuple-element.50), channel_id=1, source_target_pairs={{0,2},{3,1},{4,6},{7,5},{8,10},{11,9},{12,14},{15,13},{16,18},{19,... | collective-permute-start | bytes 3932168 | tf_op jit(solution)/shard_map/ppermute | solution.py:360
  202.7 40.8 %collective-permute-start.11 = (bf16[128,5120]{1,0:T(8,128)(2,1)}, bf16[128,5120]{1,0:T(8,128)(2,1)}, u32[]{:S(2)}, u32[]{:S(2)}) collective-permute-start(bf16[128,5120]{1,0:T(8,128)(2,1)} %collective-permute-done.8.refs_0_), channel_id=1, source_target_pairs={{1,0},{2,3},{5,4},{6,7},{9,8},{10,11},{13,12},{14,15},{17,16},{18,... | collective-permute-start | bytes 3932168 | tf_op jit(solution)/shard_map/ppermute | solution.py:360
  204.1 1.3 copy-start.8
  205.4 1.1 copy-start.10
  227.6 36.5 %collective-permute-start.13 = (bf16[128,5120]{1,0:T(8,128)(2,1)}, bf16[128,5120]{1,0:T(8,128)(2,1)}, u32[]{:S(2)}, u32[]{:S(2)}) collective-permute-start(bf16[128,5120]{1,0:T(8,128)(2,1)} %collective-permute-done.12.refs_1_), channel_id=1, source_target_pairs={{1,0},{2,3},{5,4},{6,7},{9,8},{10,11},{13,12},{14,15},{17,16},{18,... | collective-permute-start | bytes 3932168 | tf_op jit(solution)/shard_map/ppermute | solution.py:360
  229.9 1.3 copy-start.5
  231.3 32.9 %copy-start.1 = (bf16[1280,1536]{1,0:T(8,128)(2,1)S(1)}, bf16[1280,1536]{1,0:T(8,128)(2,1)}, u32[]{:S(2)}) copy-start(bf16[1280,1536]{1,0:T(8,128)(2,1)} %all-gather.7.cloned.1.call-done.refs_9_.refs_5_) | copy-start | bytes 11796484
  231.3 32.9 %copy-start.2 = (bf16[1280,1536]{1,0:T(8,128)(2,1)S(1)}, bf16[1280,1536]{1,0:T(8,128)(2,1)}, u32[]{:S(2)}) copy-start(bf16[1280,1536]{1,0:T(8,128)(2,1)} %all-gather.9.cloned.1.call-done.refs_10_.refs_6_) | copy-start | bytes 11796484
  243.5 20.7 %copy-start = (bf16[1280,1536]{1,0:T(8,128)(2,1)S(1)}, bf16[1280,1536]{1,0:T(8,128)(2,1)}, u32[]{:S(2)}) copy-start(bf16[1280,1536]{1,0:T(8,128)(2,1)} %all-gather.5.cloned.1.call-done.refs_8_.refs_4_) | copy-start | bytes 11796484
  243.5 1.3 copy-start.6
  244.8 1.5 copy-start.11
  264.2 2.1 copy-start.3
Sparse Core Ops, SparseCore 0:
  12.5 33.9 all-gather.4
  94.7 38.8 all-gather.6
  135.2 32.9 all-gather.8
  169.6 32.9 all-gather.10
